TPU v7x, 256 devices: a whole 4x4x8 slice. The times are simulated.
256 devices in a mesh: ctx: 32 (over z, x_hi, core), dp: 8 (over y, x_lo).
Axes of the slice: x: 4 (x_hi: 2, x_lo: 2; x = x_hi * 2 + x_lo), y: 4, z: 8, core: 2. Of those that a mesh axis runs over, the one named last changes fastest.
Arguments:
- latent_values: bfloat16 [8, 4096, 576], P('dp', 'ctx'), may hold values from -6 to 6, as said below
- latent_exponents: int32 [8, 32, 9], P('dp', 'ctx'), may hold values from -1 to 1
- query_nope: bfloat16 [8, 4096, 512], P('dp', 'ctx'), may hold values from -6 to 6
- query_rope: bfloat16 [8, 4096, 256], P('dp', 'ctx'), may hold values from -480 to 480
- key_up: bfloat16 [512, 512], replicated, may hold values from -0.5 to 0.5
- value_up: bfloat16 [512, 512], replicated, may hold values from -0.25 to 0.25
- cotangent: bfloat16 [8, 4096, 512], P('dp', 'ctx'), may hold values from -6 to 6
Outputs:
- attended: bfloat16 [8, 4096, 512], P('dp', 'ctx')
- grad_query_nope: bfloat16 [8, 4096, 512], P('dp', 'ctx')
- grad_query_rope: bfloat16 [8, 4096, 256], P('dp', 'ctx')
- grad_latent: float32 [8, 4096, 576], P('dp', 'ctx')
- grad_weights: float32 [512, 1024], P('ctx', 'dp')
Inputs may be any that keep to these rules, and one draw needn't show every extreme that they name: `latent_values`: the last 64 columns of every position are the rotary key, which may be closely aligned with the rotary queries of some positions, so that scores can be large; entries lie in the stated range.
All inputs are finite; a program needn't handle non-finite values.
Results may differ from a plain program's by a relative error of at most 0.025.
Values may be sent and summed in bfloat16 or wider, within the bound.
A program may use at most 128 MiB of HBM per device.

v0:
```python
import jax
import jax.numpy as jnp
from jax import lax
from jax.sharding import PartitionSpec as P

LATENT = 512
ROPE = 64
NOPE = 128
VDIM = 128
HEADS = 4


def shards(latent_values, latent_exponents, query_nope, query_rope, key_up, value_up, cotangent):
    rows = latent_values.shape[1]
    width = latent_values.shape[2]
    heads = HEADS
    factor = (NOPE + ROPE) ** (-0.5)
    first_row = lax.axis_index("ctx") * rows
    last_row = first_row + rows - 1
    total = rows * lax.axis_size("ctx")
    factors = jnp.exp2(latent_exponents[0].astype(jnp.float32))
    blocks = factors.shape[0]
    groups = factors.shape[1]

    def expand(values):
        shaped = values.reshape(blocks, rows // blocks, groups, width // groups)
        return (shaped * factors[:, None, :, None]).reshape(rows, width)

    latent_rows = expand(latent_values[0].astype(jnp.float32)).astype(jnp.bfloat16)
    query_three = query_nope[0].reshape(rows, heads, NOPE)
    key_three = key_up.reshape(LATENT, heads, NOPE)
    value_three = value_up.reshape(LATENT, heads, VDIM)
    qlat = jnp.einsum(
        "the,dhe->thd", query_three, key_three, preferred_element_type=jnp.float32
    ).astype(jnp.bfloat16)
    qall = jnp.concatenate([qlat, query_rope[0].reshape(rows, heads, ROPE)], axis=-1).reshape(
        rows * heads, width
    )
    qpos = first_row + jnp.arange(rows * heads) // heads

    def scores_of(piece):
        raw = jnp.dot(qall, piece.T, preferred_element_type=jnp.float32) * factor
        kpos = jnp.arange(piece.shape[0])
        return jnp.where(kpos[None, :] <= qpos[:, None], raw, -jnp.inf)

    stats_init = (
        jnp.full((rows * heads,), -1e30, jnp.float32),
        jnp.zeros((rows * heads,), jnp.float32),
    )

    def run_back(lse, dolat, delta, carry, piece, start):

        def work(state):
            prob = jnp.exp(scores_of(piece) - lse[:, None])
            weights = prob.astype(jnp.bfloat16)
            dprob = jnp.dot(dolat, piece[:, :LATENT].T, preferred_element_type=jnp.float32)
            dscore = (prob * (dprob - delta[:, None]) * factor).astype(jnp.bfloat16)
            dq = jnp.dot(dscore, piece, preferred_element_type=jnp.float32)
            term = jnp.einsum("rk,rd->kd", dscore, qall, preferred_element_type=jnp.float32)
            term_nope = jnp.einsum("rk,rd->kd", weights, dolat, preferred_element_type=jnp.float32)
            term = term.at[:, :LATENT].add(term_nope)
            return (dq, term)

        return lax.cond(start <= last_row, work, lambda state: state, carry)

    back_init = (
        jnp.zeros((rows * heads, width), jnp.float32),
        jnp.zeros((total, width), jnp.float32),
    )
    mix_init = jnp.zeros((rows * heads, LATENT), jnp.float32)
    piece = lax.all_gather(latent_rows, "ctx", axis=0, tiled=True)

    def work(state):
        scores = scores_of(piece)
        newtop = jnp.maximum(state[0], jnp.max(scores, axis=1))
        summed = jnp.sum(jnp.exp(scores - newtop[:, None]), axis=1)
        return (newtop, summed)

    stats = lax.cond(jnp.int32(0) <= last_row, work, lambda state: state, stats_init)
    lse = stats[0] + jnp.log(stats[1])
    run_piece = lax.all_gather(latent_rows, "ctx", axis=0, tiled=True)

    def work(acc):
        weights = jnp.exp(scores_of(run_piece) - lse[:, None]).astype(jnp.bfloat16)
        return jnp.dot(weights, run_piece[:, :LATENT], preferred_element_type=jnp.float32)

    mixed = lax.cond(jnp.int32(0) <= last_row, work, lambda acc: acc, mix_init)
    olat = mixed.astype(jnp.bfloat16)
    olat_three = olat.reshape(rows, heads, LATENT)
    attended = jnp.einsum(
        "thd,dhe->the", olat_three, value_three, preferred_element_type=jnp.float32
    ).astype(jnp.bfloat16)
    cot_three = cotangent[0].reshape(rows, heads, VDIM)
    dolat = (
        jnp.einsum("the,dhe->thd", cot_three, value_three, preferred_element_type=jnp.float32)
        .astype(jnp.bfloat16)
        .reshape(rows * heads, LATENT)
    )
    delta = jnp.sum(dolat.astype(jnp.float32) * olat.astype(jnp.float32), axis=1)
    olat_three, attended, cot_three, dolat, delta = (olat_three, attended, cot_three, dolat, delta)
    backed = run_back(
        lse,
        dolat,
        delta,
        back_init,
        lax.all_gather(latent_rows, "ctx", axis=0, tiled=True),
        jnp.int32(0),
    )
    dq_all = backed[0].reshape(rows, heads, width)
    own_terms = lax.psum_scatter(
        backed[1].astype(jnp.bfloat16), "ctx", scatter_dimension=0, tiled=True
    ).astype(jnp.float32)
    grad_latent = expand(own_terms)
    dqlat = dq_all[..., :LATENT].astype(jnp.bfloat16)
    grad_rope = dq_all[..., LATENT:].astype(jnp.bfloat16).reshape(1, rows, heads * ROPE)
    grad_nope = (
        jnp.einsum("thd,dhe->the", dqlat, key_three, preferred_element_type=jnp.float32)
        .astype(jnp.bfloat16)
        .reshape(1, rows, heads * NOPE)
    )
    grad_key = jnp.einsum(
        "thd,the->dhe", dqlat, query_three, preferred_element_type=jnp.float32
    ).reshape(LATENT, heads * NOPE)
    grad_value = jnp.einsum(
        "thd,the->dhe", olat_three, cot_three, preferred_element_type=jnp.float32
    ).reshape(LATENT, heads * VDIM)
    partial_sum = jnp.concatenate([grad_key, grad_value], axis=1)
    summed_rows = lax.psum_scatter(
        partial_sum.astype(jnp.bfloat16), "ctx", scatter_dimension=0, tiled=True
    )
    grad_weights = lax.psum_scatter(summed_rows, "dp", scatter_dimension=1, tiled=True).astype(
        jnp.float32
    )
    return (
        attended.reshape(1, rows, heads * VDIM),
        grad_nope,
        grad_rope,
        grad_latent[None],
        grad_weights,
    )


def solution(mesh):
    placed = (
        P("dp", "ctx", None),
        P("dp", "ctx", None),
        P("dp", "ctx", None),
        P("dp", "ctx", None),
        P(),
        P(),
        P("dp", "ctx", None),
    )
    return jax.shard_map(
        shards,
        mesh=mesh,
        in_specs=placed,
        out_specs=(
            P("dp", "ctx", None),
            P("dp", "ctx", None),
            P("dp", "ctx", None),
            P("dp", "ctx", None),
            P("ctx", "dp"),
        ),
        check_vma=False,
    )
```

profile of v0, /device:TPU:4, one launch (start us, length us, event | category | flops | bytes accessed | tf_op | source)
XLA Modules:
  0.0 490.1 jit_solution(182419815269694162)
XLA Ops:
  8.1 1.7 fusion.17
  12.9 1.3 copy.94
  15.2 1.1 fusion.12
  16.3 85.1 %all-gather.2.cloned.1.call-done = bf16[4096,576]{0,1:T(8,128)(2,1)} async-done(((bf16[128,576]{0,1:T(8,128)(2,1)}), bf16[4096,576]{0,1:T(8,128)(2,1)}) %all-gather.2.cloned.1.call-update) | async-done | bytes 4718608 | tf_op jit(solution)/shard_map/all_gather | solution.py:81
  101.3 9.8 %conditional.3 = (f32[512]{0:T(512)}, f32[512]{0:T(512)S(1)}) conditional(s32[]{:T(128)} %convert_element_type.94, () %tuple.49, (s32[512]{0:T(512)S(1)}, bf16[512,576]{1,0:T(8,128)(2,1)S(1)}, bf16[4096,576]{0,1:T(8,128)(2,1)}) %tuple.50), branch_computations={%region_0.1_spmd, %region_1.4_spmd} | conditional | flops 2434792960 | bytes 22104080 | solution.py:79
  101.3 5.9 %fusion = (f32[512]{0:T(512)S(1)}, f32[512,4096]{1,0:T(8,128)S(1)}) fusion(s32[512]{0:T(512)S(1)} %get-tuple-element.75, bf16[512,576]{1,0:T(8,128)(2,1)S(1)} %get-tuple-element.76, bf16[4096,576]{0,1:T(8,128)(2,1)} %get-tuple-element.158), kind=kOutput, calls=%fused_computation.3 | convolution fusion | flops 2424307200 | bytes 13701120 | tf_op jit(solution)/shard_map/cond/branch_1_fun/dot_general | solution.py:42
  107.8 3.4 exponential_reduce_fusion
  111.8 19.5 %conditional.4 = (bf16[512,512]{1,0:T(8,128)(2,1)}, bf16[128,4,512]{2,0,1:T(8,128)(2,1)S(1)}) conditional(s32[]{:T(128)} %convert_element_type.94, () %tuple.48, (s32[512]{0:T(512)S(1)}, bf16[512,576]{1,0:T(8,128)(2,1)S(1)}, bf16[4096,576]{0,1:T(8,128)(2,1)}, f32[512]{0:T(512)S(1)}) %tuple.51), branch_computations={%region_4.5_spmd, %region_5.6_spmd} | conditional | flops 4574150656 | bytes 21565456 | solution.py:87
  111.8 7.6 %copy.63 = bf16[4096,576]{1,0:T(8,128)(2,1)} copy(bf16[4096,576]{0,1:T(8,128)(2,1)} %get-tuple-element.161) | data formatting | bytes 9437184 | tf_op jit(solution)/shard_map
  119.5 10.6 %fusion.3 = bf16[512,512]{1,0:T(8,128)(2,1)} fusion(bf16[4096,576]{1,0:T(8,128)(2,1)} %copy.63, bf16[512,576]{1,0:T(8,128)(2,1)S(1)} %get-tuple-element.79, bf16[4096,576]{0,1:T(8,128)(2,1)} %get-tuple-element.161, f32[512]{0:T(512)S(1)} %get-tuple-element.81, s32[512]{0:T(512)S(1)} %get-tuple-element.78), kind=kOutput, calls=%fused_computation.9 | convolution fusion | flops 4574150656 | bytes 10031104 | tf_op jit(solution)/shard_map/cond/branch_1_fun/dot_general | solution.py:85
  130.0 1.2 reshape.112
  132.6 56.9 %conditional.5 = (f32[4096,576]{0,1:T(8,128)}, bf16[128,4,512]{2,0,1:T(8,128)(2,1)S(1)}, bf16[1,128,256]{2,1,0:T(8,128)(2,1)S(1)}) conditional(s32[]{:T(128)} %convert_element_type.94, () %tuple.52, (s32[512]{0:T(512)S(1)}, bf16[512,576]{1,0:T(8,128)(2,1)S(1)}, bf16[4096,576]{0,1:T(8,128)(2,1)}, f32[512]{0:T(512)S(1)}, ...), branch_computations={%region_6.7_spmd.clone, %region_7.10_spmd.clone} | conditional | flops 11567136768 | bytes 189866720 | solution.py:64
  133.4 1.4 copy.69
  135.0 1.3 multiply_reduce_fusion
  136.2 7.7 %copy.68 = bf16[4096,576]{1,0:T(8,128)(2,1)} copy(bf16[4096,576]{0,1:T(8,128)(2,1)} %get-tuple-element.165) | data formatting | bytes 9437184 | tf_op jit(solution)/shard_map
  143.9 6.6 %subtract_exponential_fusion = f32[512,4096]{1,0:T(8,128)S(1)} fusion(bf16[512,576]{1,0:T(8,128)(2,1)} %copy-done.3, bf16[4096,576]{0,1:T(8,128)(2,1)} %get-tuple-element.165, f32[512]{0:T(512)S(1)} %get-tuple-element.114, s32[512]{0:T(512)S(1)} %get-tuple-element.111), kind=kOutput, calls=%fused_computation.15 | convolution fusion | flops 2424307712 | bytes 13701120 | tf_op jit(solution)/shard_map/cond/branch_1_fun/dot_general | solution.py:42
  150.6 7.7 %multiply_convert_fusion = bf16[512,4096]{1,0:T(8,128)(2,1)S(1)} fusion(f32[512,4096]{1,0:T(8,128)S(1)} %subtract_exponential_fusion, bf16[512,512]{1,0:T(8,128)(2,1)S(1)} %reshape.136, bf16[4096,576]{1,0:T(8,128)(2,1)} %copy.68, f32[512]{0:T(512)S(1)} %multiply_reduce_fusion), kind=kOutput, calls=%fused_computation.14 | convolution fusion | flops 2155872256 | bytes 17303552 | tf_op jit(solution)/shard_map/cond/branch_1_fun/dot_general | solution.py:56
  158.3 2.0 copy-done.2
  160.3 3.6 convolution_convert_fusion
  163.9 2.1 copy.57
  166.1 2.3 reshape.139
  169.3 1.2 slice.52
  170.9 8.8 %fusion.22 = f32[4096,576]{0,1:T(8,128)} fusion(bf16[512,4096]{1,0:T(8,128)(2,1)} %copy-done.2, bf16[512,576]{1,0:T(8,128)(2,1)} %copy-done.3), kind=kOutput, calls=%fused_computation.49 | convolution fusion | flops 2415919104 | bytes 14221312 | tf_op jit(solution)/shard_map/cond/branch_1_fun/rk,rd->kd/dot_general | solution.py:59
  179.7 9.7 %fusion.8 = f32[4096,576]{0,1:T(8,128)} fusion(f32[4096,576]{0,1:T(8,128)} %fusion.22, bf16[512,512]{1,0:T(8,128)(2,1)S(1)} %reshape.136, f32[512,4096]{1,0:T(8,128)S(1)} %bitcast.65, pred[]{:T(512)} %compare_reduce_fusion), kind=kOutput, calls=%fused_computation.13 | convolution fusion | flops 2153775104 | bytes 25690624 | tf_op jit(solution)/shard_map/cond/branch_1_fun/rk,rd->kd/dot_general | solution.py:60
  189.9 2.1 pad_maximum_fusion
  192.1 113.3 %reduce-scatter.8.cloned.1.call-done = bf16[16,1024]{1,0:T(8,128)(2,1)} async-done(((bf16[512,1024]{1,0:T(8,128)(2,1)}), bf16[16,1024]{1,0:T(8,128)(2,1)}) %reduce-scatter.8.cloned.1.call-update) | async-done | bytes 32784 | tf_op jit(solution)/shard_map/reduce_scatter | solution.py:128
  305.5 1.6 copy.86
  307.1 6.6 %convert_element_type.107 = bf16[4096,576]{0,1:T(8,128)(2,1)} convert(f32[4096,576]{0,1:T(8,128)} %get-tuple-element.104) | non-fusion elementwise | flops 2359296 | bytes 14155776 | tf_op jit(solution)/shard_map/convert_element_type | solution.py:111
  313.7 7.6 %copy.84 = bf16[4096,576]{1,0:T(8,128)(2,1)} copy(bf16[4096,576]{0,1:T(8,128)(2,1)} %convert_element_type.107) | data formatting | bytes 9437184
  323.6 23.9 %reduce-scatter.12.cloned.1.call-done = bf16[128,16]{1,0:T(8,128)(2,1)} async-done(((bf16[1024,16]{1,0:T(8,128)(2,1)}), bf16[128,16]{1,0:T(8,128)(2,1)}) %reduce-scatter.12.cloned.1.call-update) | async-done | bytes 4112
  348.9 132.7 %reduce-scatter.10.cloned.1.call-done = bf16[128,576]{1,0:T(8,128)(2,1)} async-done(((bf16[4096,576]{1,0:T(8,128)(2,1)}), bf16[128,576]{1,0:T(8,128)(2,1)}) %reduce-scatter.10.cloned.1.call-update) | async-done | bytes 147472
  481.7 1.1 copy.85
  (60 shorter events, 14.9 us)
Async XLA Ops:
  7.2 8.0 %copy-start = (bf16[512,512]{1,0:T(8,128)(2,1)S(1)}, bf16[512,512]{1,0:T(8,128)(2,1)}, u32[]{:S(2)}) copy-start(bf16[512,512]{1,0:T(8,128)(2,1)} %param.20) | copy-start | bytes 1572868
  7.2 94.1 %all-gather.2.cloned.1.call-start = ((), (), s32[]{:S(2)}) async-start(), calls=%async_computation.3 | async-start | bytes 4866048 | tf_op jit(solution)/shard_map/all_gather | solution.py:81
  9.8 295.6 %reduce-scatter.8.cloned.1.call-start = ((), (), s32[]{:S(2)}) async-start(), calls=%async_computation.4 | async-start | bytes 1081344 | tf_op jit(solution)/shard_map/reduce_scatter | solution.py:128
  132.6 0.8 copy-start.3
  136.2 24.1 %slice-start.2 = ((s8[4718592]{0:T(1024)(128)(4,1)}), s8[524288]{0:T(1024)(128)(4,1)S(1)}, s32[]{:S(2)}) async-start(s8[4718592]{0:T(1024)(128)(4,1)} %bitcast.66), calls=%async_computation.9 | async-start | bytes 1048576 | tf_op jit(solution)/shard_map/cond
  143.9 16.4 %slice-start.3 = ((s8[4718592]{0:T(1024)(128)(4,1)}), s8[4194304]{0:T(1024)(128)(4,1)S(1)}, s32[]{:S(2)}) async-start(s8[4718592]{0:T(1024)(128)(4,1)} %bitcast.66), calls=%async_computation.10 | async-start | bytes 8388608 | tf_op jit(solution)/shard_map/cond
  150.6 7.7 %copy-start.1 = (f32[512,4096]{1,0:T(8,128)}, f32[512,4096]{1,0:T(8,128)S(1)}, u32[]{:S(2)}) copy-start(f32[512,4096]{1,0:T(8,128)S(1)} %subtract_exponential_fusion) | copy-start | bytes 25165828 | tf_op jit(solution)/shard_map/cond
  158.3 2.0 copy-start.2
  170.8 8.9 %slice-start = ((s8[8388608]{0:T(1024)(128)(4,1)}), s8[4194304]{0:T(1024)(128)(4,1)S(1)}, s32[]{:S(2)}) async-start(s8[8388608]{0:T(1024)(128)(4,1)} %bitcast.64), calls=%async_computation.7 | async-start | bytes 8388608 | tf_op jit(solution)/shard_map/cond
  170.9 8.8 %slice-start.1 = ((s8[8388608]{0:T(1024)(128)(4,1)}), s8[4194304]{0:T(1024)(128)(4,1)S(1)}, s32[]{:S(2)}) async-start(s8[8388608]{0:T(1024)(128)(4,1)} %bitcast.64), calls=%async_computation.8 | async-start | bytes 8388608 | tf_op jit(solution)/shard_map/cond
  189.4 124.3 %copy-start.4 = (bf16[1,128,256]{2,1,0:T(8,128)(2,1)}, bf16[1,128,256]{2,1,0:T(8,128)(2,1)S(1)}, u32[]{:S(2)}) copy-start(bf16[1,128,256]{2,1,0:T(8,128)(2,1)S(1)} %get-tuple-element.176) | copy-start | bytes 196612
  192.1 155.4 %reduce-scatter.12.cloned.1.call-start = ((), (), s32[]{:S(2)}) async-start(), calls=%async_computation.6 | async-start | bytes 294912
  307.1 174.6 %reduce-scatter.10.cloned.1.call-start = ((), (), s32[]{:S(2)}) async-start(), calls=%async_computation.5 | async-start | bytes 5406720
Sparse Core Ops, SparseCore 0:
  11.2 90.1 all-gather.1
  192.2 113.2 reduce-scatter.7
  308.7 38.7 reduce-scatter.11
  351.6 130.0 reduce-scatter.9
where the time goes:
time: 493 us; the launch traced here: 490 us
  waiting for transfers between devices  355 us (72%)
  matrix products  55.5 us (11%)
  local copies, waits for them, and re-layouts  46.1 us (9%)
  other arithmetic  19.2 us (4%)
  between operations  13.9 us (3%)
    unnamed x6, waiting for transfers between devices  157 us
    reduce_scatter x1, waiting for transfers between devices, shards(): lax.psum_scatter(partial_sum.astype(jnp.bfloat16), 'ctx', scatter_dimensi...  113 us
    all_gather x1, waiting for transfers between devices, shards(): run_piece = lax.all_gather(latent_rows, 'ctx', axis=0, tiled=True)  85.1 us
    another operation x5, local copies, waits for them, and re-layouts  21.2 us
    unnamed x11, local copies, waits for them, and re-layouts  12.7 us
    dot_general x2, matrix products, scores_of(): raw = jnp.dot(qall, piece.T, preferred_element_type=jnp.float32) * factor  12.5 us
    dot_general x1, matrix products, work(): jnp.dot(weights, run_piece[:, :LATENT], preferred_element_type=jnp.float32)  10.6 us
  transfers between devices with their start and end apart: 4, of which 4 were waited for; matrix products, arithmetic and copies ran while one was open for 5% of the time, Pallas kernels for 0%

commit v1 on v0

v1 whole, which is shorter than its diff:
```python
import math

import jax
import jax.numpy as jnp
from jax import lax
from jax.experimental import pallas as pl
from jax.experimental.pallas import tpu as pltpu
from jax.sharding import PartitionSpec as P

LATENT = 512
ROPE = 64
WIDTH = LATENT + ROPE
HEADS = 4
HEAD = 128
ROWS = 128
HALF = ROWS * HEADS
QROWS = 2 * HALF
Z = 8
KEYS = 2 * ROWS
FACTOR = (HEAD + ROPE) ** -0.5
LOG2E = math.log2(math.e)
NEG = -1e30
PARTS = 2
PROWS = ROWS // PARTS
BF16 = jnp.bfloat16
F32 = jnp.float32


def dot(a, b):
    return jnp.dot(a, b, preferred_element_type=F32)


def transposed(a):
    return a.astype(F32).T.astype(BF16)


def remote(src, dst, send, recv, device):
    return pltpu.make_async_remote_copy(
        src_ref=src,
        dst_ref=dst,
        send_sem=send,
        recv_sem=recv,
        device_id=device,
        device_id_type=pl.DeviceIdType.MESH,
    )


def kernel(
    lat_ref, exp_ref, qn_ref, qr_ref, ku_ref, vu_ref, ct_ref,
    att_ref, gn_ref, gr_ref, gl_ref, gw_ref,
    kv, kt, pqn, pqr, pct, q, qt, do, dot_t, kut, vut,
    s_ref, dp_ref, w_ref, ds_ref, acc, dq, ot, st, pst, fin,
    aown, asend, arecv, gown, gsend, grecv,
    dl, pr, sdn, sup, rdn, rup,
    wg, wa, wb, rb, wc, rc, wd, rd,
    up_s, up_r, dn_s, dn_r, sib_s, sib_r, pq_s, pq_r, mid_s, mid_r,
    ls_s, ls_r, rdn_s, rdn_r, rup_s, rup_r,
    a_s, a_r, b_s, b_r, c_s, c_r, d_s, d_r,
):
    k = lax.axis_index("ctx")
    p = lax.axis_index("dp")
    z, xh, c = k // 4, lax.rem(k // 2, 2), lax.rem(k, 2)
    y, xl = p // 2, lax.rem(p, 2)
    x = xh * 2 + xl

    def at(z_, x_, c_, y_):
        return (z_ * 4 + (x_ // 2) * 2 + c_, y_ * 2 + lax.rem(x_, 2))

    sibling = at(z, x, 1 - c, y)
    partner = at(z, lax.rem(x + 2, 4), c, y)
    above = at(lax.rem(z + 1, Z), x, c, y)
    below = at(lax.rem(z + Z - 1, Z), x, c, y)
    xpeers = [lax.rem(x + d, 4) for d in (1, 2, 3)]
    ypeers = [lax.rem(y + d, 4) for d in (1, 2, 3)]
    zpeers = [lax.rem(z + d, Z) for d in range(1, Z)]

    barrier = pltpu.get_barrier_semaphore()
    peers = [sibling]
    peers += [at(z, v, c, y) for v in xpeers]
    peers += [at(z, x, c, v) for v in ypeers]
    peers += [at(v, x, c, y) for v in zpeers]
    for peer in peers:
        pl.semaphore_signal(barrier, inc=1, device_id=peer, device_id_type=pl.DeviceIdType.MESH)

    st[...] = jnp.zeros_like(st)

    group = lax.broadcasted_iota(jnp.int32, (1, WIDTH), 1) // 64
    exps = jnp.zeros((1, WIDTH), jnp.int32)
    for g in range(WIDTH // 64):
        exps = jnp.where(group == g, exp_ref[0, 0, g], exps)
    scale = jnp.where(exps > 0, 2.0, jnp.where(exps < 0, 0.5, 1.0)).astype(F32)
    kv[z, c] = (lat_ref[0].astype(F32) * scale).astype(BF16)

    pl.semaphore_wait(barrier, len(peers))

    def piece(h):
        return pl.ds(h * PROWS, PROWS)

    def up_copy(block, s, h):
        ref = kv.at[block, c, piece(h)]
        return remote(ref, ref, up_s.at[s - 1, h], up_r.at[s - 1, h], above)

    def dn_copy(block, s, h):
        ref = kv.at[block, c, piece(h)]
        return remote(ref, ref, dn_s.at[s - 1, h], dn_r.at[s - 1, h], below)

    def sib_copy(block, i):
        ref = kv.at[block, c]
        return remote(ref, ref, sib_s.at[i], sib_r.at[i], sibling)

    def up_sent(s):
        return (z <= Z - 2) & (z >= s - 1), jnp.maximum(z - (s - 1), 0)

    def dn_sent(s):
        block = lax.rem(z + s - 1, Z)
        return block <= 2, block

    def up_got(s):
        return z >= s, jnp.maximum(z - s, 0)

    def dn_got(s):
        block = lax.rem(z + s, Z)
        return block <= 2, block

    def dn_used(s):
        return z >= Z - s, jnp.maximum(z + s - Z, 0)

    def send_up(s, h):
        ok, block = up_sent(s)

        @pl.when(ok)
        def _():
            up_copy(block, s, h).start()

    def send_dn(s, h):
        ok, block = dn_sent(s)

        @pl.when(ok)
        def _():
            dn_copy(block, s, h).start()

    for h in range(PARTS):
        send_up(1, h)
        send_dn(1, h)
    sib_copy(z, 0).start()
    query_copies = [
        remote(src.at[0], dst, pq_s.at[i], pq_r.at[i], partner)
        for i, (src, dst) in enumerate(((qn_ref, pqn), (qr_ref, pqr), (ct_ref, pct)))
    ]
    for copy in query_copies:
        copy.start()

    for h in range(HEADS):
        cols = pl.ds(h * HEAD, HEAD)
        kut[cols, :] = transposed(ku_ref[:, cols])
        vut[cols, :] = transposed(vu_ref[:, cols])

    def tables(half, qn, qr, ct):
        rope_t = qr.astype(F32).T
        for h in range(HEADS):
            cols = pl.ds(h * HEAD, HEAD)
            rows = pl.ds(half * HALF + h * HEAD, HEAD)
            qh = qn[:, h * HEAD:(h + 1) * HEAD]
            ch = ct[:, h * HEAD:(h + 1) * HEAD]
            rope_h = rope_t[h * ROPE:(h + 1) * ROPE, :]
            q[rows, pl.ds(0, LATENT)] = dot(qh, kut[cols, :]).astype(BF16)
            q[rows, pl.ds(LATENT, ROPE)] = rope_h.T.astype(BF16)
            qt[pl.ds(0, LATENT), rows] = dot(ku_ref[:, cols], transposed(qh)).astype(BF16)
            qt[pl.ds(LATENT, ROPE), rows] = rope_h.astype(BF16)
            do[rows, :] = dot(ch, vut[cols, :]).astype(BF16)
            dot_t[:, rows] = dot(vu_ref[:, cols], transposed(ch)).astype(BF16)

    tables(0, qn_ref[0], qr_ref[0], ct_ref[0])

    def turn(block):
        kt[block] = transposed(kv[block].reshape(KEYS, WIDTH))

    def forward(block, start, count, first):
        rows = pl.ds(start, count)
        keys = kv[block].reshape(KEYS, WIDTH)
        score = dot(keys, qt[:, rows]) * (FACTOR * LOG2E)
        if first:
            kpos = lax.broadcasted_iota(jnp.int32, (KEYS, count), 0) + xh * KEYS
            lane = lax.rem(lax.broadcasted_iota(jnp.int32, (KEYS, count), 1), ROWS)
            qx = xh if start == 0 else 1 - xh
            score = jnp.where(kpos <= lane + (qx * KEYS + c * ROWS), score, NEG)
        dprob = dot(keys[:, :LATENT], dot_t[:, rows])
        s_ref[block, :, rows] = score
        dp_ref[block, :, rows] = dprob
        top = jnp.max(score, axis=0, keepdims=True)
        if not first:
            old = st[0:1, rows]
            top = jnp.maximum(old, top)
            decay = jnp.exp2(old - top)
        e = jnp.exp2(score - top)
        total = jnp.sum(e, axis=0, keepdims=True)
        delta = jnp.sum(e * dprob, axis=0, keepdims=True)
        mixed = dot(kt[block, pl.ds(0, LATENT)], e.astype(BF16))
        if not first:
            total += st[1:2, rows] * decay
            delta += st[2:3, rows] * decay
            mixed += acc[:, rows] * decay
        st[0:1, rows] = top
        st[1:2, rows] = total
        st[2:3, rows] = delta
        acc[:, rows] = mixed

    def blocks_of(s):
        used, low = dn_used(s)
        count = (z >= s).astype(jnp.int32)
        if s <= 3:
            count += used.astype(jnp.int32)
        high = jnp.maximum(z - s, 0)
        return count, lambda i: jnp.where(i == 0, high, low)

    def forward_step(s, start, count, new):
        blocks, nth = blocks_of(s)

        def body(i, carry):
            if new:
                turn(nth(i))
            forward(nth(i), start, count, False)
            return carry

        lax.fori_loop(0, blocks, body, 0)

    def relay(s):
        for h in range(PARTS):
            got, block = up_got(s)

            @pl.when(got)
            def _():
                up_copy(block, s, h).wait_recv()

            if s < 4:
                send_up(s + 1, h)
            if s <= 3:
                got_dn, block_dn = dn_got(s)

                @pl.when(got_dn)
                def _():
                    dn_copy(block_dn, s, h).wait_recv()

                if s < 3:
                    send_dn(s + 1, h)
        got, block = up_got(s)

        @pl.when(got)
        def _():
            sib_copy(block, s).start()

        if s <= 3:
            used, low = dn_used(s)

            @pl.when(used)
            def _():
                sib_copy(low, 4 + s).start()

    def meet(s):
        got, block = up_got(s)

        @pl.when(got)
        def _():
            sib_copy(block, s).wait_recv()

        if s <= 3:
            used, low = dn_used(s)

            @pl.when(used)
            def _():
                sib_copy(low, 4 + s).wait_recv()

    sib_copy(z, 0).wait_recv()
    turn(z)
    forward(z, 0, HALF, True)
    relay(1)
    meet(1)
    forward_step(1, 0, HALF, True)
    relay(2)
    for copy in query_copies:
        copy.wait_recv()
    tables(1, pqn[...], pqr[...], pct[...])
    forward(z, HALF, HALF, True)
    forward_step(1, HALF, HALF, False)
    relay(3)
    meet(2)
    forward_step(2, 0, QROWS, True)
    relay(4)
    meet(3)
    forward_step(3, 0, QROWS, True)
    meet(4)
    forward_step(4, 0, QROWS, True)

    stats = remote(st, pst, mid_s.at[0], mid_r.at[0], partner)
    stats.start()
    dq[...] = jnp.zeros_like(dq)
    stats.wait_recv()
    for half in range(2):
        rows, other = pl.ds(half * HALF, HALF), pl.ds((1 - half) * HALF, HALF)
        top1, top2 = st[0:1, rows], pst[0:1, other]
        top = jnp.maximum(top1, top2)
        part1, part2 = jnp.exp2(top1 - top), jnp.exp2(top2 - top)
        total = st[1:2, rows] * part1 + pst[1:2, other] * part2
        fin[0:1, rows] = top + jnp.log(total) * LOG2E
        fin[1:2, rows] = (st[2:3, rows] * part1 + pst[2:3, other] * part2) / total
        ot[:, rows] = (acc[:, rows] * (part1 / total)).astype(BF16)

    def store_terms(column, terms):
        yy, xx = column // 2, column % 2
        terms = terms.astype(BF16)
        for zz in range(Z):
            for xxh in range(2):
                for cc in range(2):
                    first = zz * 64 + xxh * 32 + cc * 16
                    wg[cc, xxh * 2 + xx, yy, zz] = terms[first:first + 16, :]

    for h in range(HEADS):
        cols = pl.ds(h * HEAD, HEAD)
        mine, theirs = pl.ds(h * HEAD, HEAD), pl.ds(HALF + h * HEAD, HEAD)
        asend[cols, :] = dot(vut[cols, :], ot[:, theirs]).astype(BF16)
        aown[cols, :] = dot(vut[cols, :], ot[:, mine])
    att_copy = remote(asend, arecv, mid_s.at[1], mid_r.at[1], partner)
    att_copy.start()
    for h in range(HEADS):
        cols = pl.ds(h * HEAD, HEAD)
        mine, theirs = pl.ds(h * HEAD, HEAD), pl.ds(HALF + h * HEAD, HEAD)
        store_terms(4 + h, dot(ot[:, mine], ct_ref[0, :, cols]) + dot(ot[:, theirs], pct[:, cols]))

    def backward(block, carry):
        prob = jnp.exp2(s_ref[block] - fin[0:1, :])
        w_ref[block] = prob.astype(BF16)
        dscore = (prob * (dp_ref[block] - fin[1:2, :]) * FACTOR).astype(BF16)
        ds_ref[block] = dscore
        dq[...] += dot(kt[block], dscore)
        return carry

    lax.fori_loop(0, z + 1, backward, 0)

    ot[...] = dq[pl.ds(0, LATENT), :].astype(BF16)
    for h in range(HEADS):
        cols = pl.ds(h * HEAD, HEAD)
        rope = pl.ds(LATENT + h * ROPE, ROPE)
        mine, theirs = pl.ds(h * HEAD, HEAD), pl.ds(HALF + h * HEAD, HEAD)
        gsend[cols, :] = dot(kut[cols, :], ot[:, theirs]).astype(BF16)
        gown[cols, :] = dot(kut[cols, :], ot[:, mine])
        gsend[rope, :] = dq[pl.ds(LATENT, ROPE), theirs].astype(BF16)
        gown[rope, :] = dq[pl.ds(LATENT, ROPE), mine]
    grad_copy = remote(gsend, grecv, mid_s.at[2], mid_r.at[2], partner)
    grad_copy.start()
    for h in range(HEADS):
        cols = pl.ds(h * HEAD, HEAD)
        mine, theirs = pl.ds(h * HEAD, HEAD), pl.ds(HALF + h * HEAD, HEAD)
        store_terms(h, dot(ot[:, mine], qn_ref[0, :, cols]) + dot(ot[:, theirs], pqn[:, cols]))
    a_copy = remote(wg.at[1 - c], wa, a_s, a_r, sibling)
    a_copy.start()

    def ls_copy(block):
        return remote(dl.at[block, 1 - c], pr.at[block], ls_s.at[block], ls_r.at[block], sibling)

    def latent_terms(block):
        a = dot(ds_ref[block], q[...])
        b = dot(w_ref[block], do[...])
        dl[block, :, :, pl.ds(0, LATENT)] = (
            (a[:, :LATENT] + b).astype(BF16).reshape(2, ROWS, LATENT)
        )
        dl[block, :, :, pl.ds(LATENT, ROPE)] = (
            a[:, LATENT:].astype(BF16).reshape(2, ROWS, ROPE)
        )
        ls_copy(block).start()

    def terms_step(t):
        high, low = z - 5 + t, z - 4 - t
        count = (high >= 0).astype(jnp.int32)
        if t <= 3:
            count += (low >= 0).astype(jnp.int32)

        def body(i, carry):
            latent_terms(jnp.where(i == 0, jnp.maximum(high, 0), jnp.maximum(low, 0)))
            return carry

        lax.fori_loop(0, count, body, 0)

    def down_copy(t, h):
        return remote(
            sdn.at[t - 1, piece(h)], rdn.at[t - 1, piece(h)],
            rdn_s.at[t - 1, h], rdn_r.at[t - 1, h], below,
        )

    def rise_copy(t, h):
        return remote(
            sup.at[t - 1, piece(h)], rup.at[t - 1, piece(h)],
            rup_s.at[t - 1, h], rup_r.at[t - 1, h], above,
        )

    def chip_sum(block, h):
        return dl[block, c, piece(h)].astype(F32) + pr[block, piece(h)].astype(F32)

    def pass_on(t):
        high, low = z - 5 + t, z - 4 - t
        goes_down = high >= 0
        high, low_block = jnp.maximum(high, 0), jnp.maximum(low, 0)

        @pl.when(goes_down)
        def _():
            ls_copy(high).wait_recv()

        if t <= 3:

            @pl.when(low >= 0)
            def _():
                ls_copy(low_block).wait_recv()

        for h in range(PARTS):

            @pl.when(goes_down)
            def _():
                if t >= 2:

                    @pl.when(z <= Z - 2)
                    def _():
                        down_copy(t - 1, h).wait_recv()
                        sdn[t - 1, piece(h)] = (
                            chip_sum(high, h) + rdn[t - 2, piece(h)].astype(F32)
                        ).astype(BF16)

                    @pl.when(z == Z - 1)
                    def _():
                        sdn[t - 1, piece(h)] = chip_sum(high, h).astype(BF16)

                else:
                    sdn[t - 1, piece(h)] = chip_sum(high, h).astype(BF16)
                down_copy(t, h).start()

            if t <= 3:

                @pl.when(low >= 0)
                def _():
                    if t >= 2:
                        rise_copy(t - 1, h).wait_recv()
                        sup[t - 1, piece(h)] = (
                            chip_sum(low_block, h) + rup[t - 2, piece(h)].astype(F32)
                        ).astype(BF16)
                    else:
                        sup[t - 1, piece(h)] = chip_sum(low_block, h).astype(BF16)
                    rise_copy(t, h).start()

                if t >= 2:

                    @pl.when(z + 4 - t <= 2)
                    def _():
                        rise_copy(t - 1, h).wait_recv()
                        sup[t - 1, piece(h)] = rup[t - 2, piece(h)]
                        rise_copy(t, h).start()

    terms_step(1)
    terms_step(2)
    pass_on(1)

    a_copy.wait_recv()
    for i in range(4):
        wb[i] = (wg[c, i].astype(F32) + wa[i].astype(F32)).astype(BF16)
    b_copies = [
        remote(wb.at[v], rb.at[i], b_s.at[i], b_r.at[i], at(z, v, c, y))
        for i, v in enumerate(xpeers)
    ]
    for copy in b_copies:
        copy.start()

    terms_step(3)
    pass_on(2)

    for copy in b_copies:
        copy.wait_recv()
    wc[...] = (
        wb[x].astype(F32) + rb[0].astype(F32) + rb[1].astype(F32) + rb[2].astype(F32)
    ).astype(BF16)
    c_copies = [
        remote(wc.at[v], rc.at[i], c_s.at[i], c_r.at[i], at(z, x, c, v))
        for i, v in enumerate(ypeers)
    ]
    for copy in c_copies:
        copy.start()

    terms_step(4)
    pass_on(3)

    for copy in c_copies:
        copy.wait_recv()
    wd[...] = (
        wc[y].astype(F32) + rc[0].astype(F32) + rc[1].astype(F32) + rc[2].astype(F32)
    ).astype(BF16)
    d_copies = [
        remote(wd.at[v], rd.at[i], d_s.at[i], d_r.at[i], at(v, x, c, y))
        for i, v in enumerate(zpeers)
    ]
    for copy in d_copies:
        copy.start()

    terms_step(5)
    pass_on(4)

    att_copy.wait_recv()
    grad_copy.wait_recv()
    for h in range(HEADS):
        cols = pl.ds(h * HEAD, HEAD)
        att_ref[0, :, cols] = (aown[cols, :] + arecv[cols, :].astype(F32)).T.astype(BF16)
        gn_ref[0, :, cols] = (gown[cols, :] + grecv[cols, :].astype(F32)).T.astype(BF16)
    for h in range(HEADS // 2):
        rows = pl.ds(LATENT + h * HEAD, HEAD)
        cols = pl.ds(h * HEAD, HEAD)
        gr_ref[0, :, cols] = (gown[rows, :] + grecv[rows, :].astype(F32)).T.astype(BF16)

    for copy in d_copies:
        copy.wait_recv()
    summed = wd[z].astype(F32)
    for i in range(Z - 1):
        summed += rd[i].astype(F32)
    gw_ref[...] = summed

    ls_copy(z).wait_recv()
    for h in range(PARTS):
        gl_ref[0, piece(h), :] = chip_sum(z, h)

        @pl.when(z <= Z - 2)
        def _():
            down_copy(4, h).wait_recv()
            gl_ref[0, piece(h), :] += rdn[3, piece(h)].astype(F32)

        @pl.when(z <= 2)
        def _():
            rise_copy(3, h).wait_recv()
            gl_ref[0, piece(h), :] += rup[2, piece(h)].astype(F32)

    gl_ref[0] = gl_ref[0] * scale

    for s in range(1, 5):
        for h in range(PARTS):
            ok, block = up_sent(s)

            @pl.when(ok)
            def _():
                up_copy(block, s, h).wait_send()

            if s <= 3:
                ok_dn, block_dn = dn_sent(s)

                @pl.when(ok_dn)
                def _():
                    dn_copy(block_dn, s, h).wait_send()

                @pl.when(lax.rem(z + 4 - s, Z) <= 2)
                def _():
                    rise_copy(s, h).wait_send()

            @pl.when(z - 5 + s >= 0)
            def _():
                down_copy(s, h).wait_send()

        got, block = up_got(s)

        @pl.when(got)
        def _():
            sib_copy(block, s).wait_send()

        if s <= 3:
            used, low = dn_used(s)

            @pl.when(used)
            def _():
                sib_copy(low, 4 + s).wait_send()

    sib_copy(z, 0).wait_send()

    def sent(block, carry):
        ls_copy(block).wait_send()
        return carry

    lax.fori_loop(0, z + 1, sent, 0)
    for copy in query_copies + [stats, att_copy, grad_copy, a_copy] + b_copies + c_copies + d_copies:
        copy.wait_send()


def shards(latent_values, latent_exponents, query_nope, query_rope, key_up, value_up, cotangent):
    dma = pltpu.SemaphoreType.DMA
    vmem = pl.BlockSpec(memory_space=pltpu.VMEM)
    scratch = [
        ((Z, 2, ROWS, WIDTH), BF16),
        ((Z, WIDTH, KEYS), BF16),
        ((ROWS, HALF), BF16),
        ((ROWS, HALF // 2), BF16),
        ((ROWS, HALF), BF16),
        ((QROWS, WIDTH), BF16),
        ((WIDTH, QROWS), BF16),
        ((QROWS, LATENT), BF16),
        ((LATENT, QROWS), BF16),
        ((HALF, LATENT), BF16),
        ((HALF, LATENT), BF16),
        ((Z, KEYS, QROWS), F32),
        ((Z, KEYS, QROWS), F32),
        ((Z, KEYS, QROWS), BF16),
        ((Z, KEYS, QROWS), BF16),
        ((LATENT, QROWS), F32),
        ((WIDTH, QROWS), F32),
        ((LATENT, QROWS), BF16),
        ((8, QROWS), F32),
        ((8, QROWS), F32),
        ((8, QROWS), F32),
        ((HALF, ROWS), F32),
        ((HALF, ROWS), BF16),
        ((HALF, ROWS), BF16),
        ((HALF + HALF // 2, ROWS), F32),
        ((HALF + HALF // 2, ROWS), BF16),
        ((HALF + HALF // 2, ROWS), BF16),
        ((Z, 2, ROWS, WIDTH), BF16),
        ((Z, ROWS, WIDTH), BF16),
        ((4, ROWS, WIDTH), BF16),
        ((3, ROWS, WIDTH), BF16),
        ((4, ROWS, WIDTH), BF16),
        ((3, ROWS, WIDTH), BF16),
        ((2, 4, 4, Z, 16, 128), BF16),
        ((4, 4, Z, 16, 128), BF16),
        ((4, 4, Z, 16, 128), BF16),
        ((3, 4, Z, 16, 128), BF16),
        ((4, Z, 16, 128), BF16),
        ((3, Z, 16, 128), BF16),
        ((Z, 16, 128), BF16),
        ((Z - 1, 16, 128), BF16),
    ]
    pairs = [
        (4, PARTS), (3, PARTS), (8,), (3,), (3,),
        (Z,), (4, PARTS), (3, PARTS),
        (), (3,), (3,), (Z - 1,),
    ]
    semaphores = []
    for shape in pairs:
        semaphores += [dma(shape) if shape else dma] * 2
    return pl.pallas_call(
        kernel,
        out_shape=(
            jax.ShapeDtypeStruct((1, ROWS, HALF), BF16),
            jax.ShapeDtypeStruct((1, ROWS, HALF), BF16),
            jax.ShapeDtypeStruct((1, ROWS, HALF // 2), BF16),
            jax.ShapeDtypeStruct((1, ROWS, WIDTH), F32),
            jax.ShapeDtypeStruct((16, 128), F32),
        ),
        in_specs=[vmem, pl.BlockSpec(memory_space=pltpu.SMEM)] + [vmem] * 5,
        out_specs=(vmem,) * 5,
        scratch_shapes=[pltpu.VMEM(*spec) for spec in scratch] + semaphores,
        compiler_params=pltpu.CompilerParams(
            collective_id=0, has_side_effects=True, vmem_limit_bytes=60 << 20
        ),
    )(latent_values, latent_exponents, query_nope, query_rope, key_up, value_up, cotangent)


def solution(mesh):
    block = P("dp", "ctx", None)
    return jax.shard_map(
        shards,
        mesh=mesh,
        in_specs=(block, block, block, block, P(), P(), block),
        out_specs=(block, block, block, block, P("ctx", "dp")),
        check_vma=False,
    )
```

time: 493 us -> 70.9 us (0.14)
  waiting for transfers between devices: 355 us -> 0 us
  Pallas kernels: 0 us -> 62.9 us
  matrix products: 55.5 us -> 0 us
  local copies, waits for them, and re-layouts: 46.1 us -> 6.7 us
  other arithmetic: 19.2 us -> 0 us
  between operations: 13.9 us -> 0.65 us
    unnamed x6 -> x0, waiting for transfers between devices: 157 us -> none
    reduce_scatter x1 -> x0, waiting for transfers between devices: 113 us -> none  [shards(): lax.psum_scatter(partial_sum.astype(jnp.bfloat16), 'ctx', scatter_dimensi...]
    all_gather x1 -> x0, waiting for transfers between devices: 85.1 us -> none  [shards(): run_piece = lax.all_gather(latent_rows, 'ctx', axis=0, tiled=True)]
    pallas_call x0 -> x1, Pallas kernels: none -> 62.9 us  [shards(): pl.pallas_call(kernel, out_shape=(jax.ShapeDtypeStruct((1, ROWS, HALF), B...]
    dot_general x13 -> x0, matrix products: 55.5 us -> none  [the longest x2 12.5 us: scores_of(): raw = jnp.dot(qall, piece.T, preferred_element_type=jnp.float32) * factor]
    another operation x7 -> x0, local copies, waits for them, and re-layouts: 23.2 us -> none
    convert_element_type x3 -> x0, other arithmetic: 8.95 us -> none  [the longest x1 6.6 us: shards(): backed[1].astype(jnp.bfloat16)]
    unnamed x11 -> x13, local copies, waits for them, and re-layouts: 12.7 us -> 4.82 us
  transfers between devices with their start and end apart: 4 -> 0, of which waited for: 4 -> 0; matrix products, arithmetic and copies ran while one was open for 5% -> 0% of each run, Pallas kernels for 0% -> 0%
where the time goes in v1:
time: 70.9 us; the launch traced here: 70.2 us
  Pallas kernels  62.9 us (89%)
  local copies, waits for them, and re-layouts  6.7 us (9%)
    pallas_call x1, Pallas kernels, shards(): pl.pallas_call(kernel, out_shape=(jax.ShapeDtypeStruct((1, ROWS, HALF), B...  62.9 us
    unnamed x13, local copies, waits for them, and re-layouts  4.82 us
    pallas_call x1, local copies, waits for them, and re-layouts, shards(): pl.pallas_call(kernel, out_shape=(jax.ShapeDtypeStruct((1, ROWS, HALF), B...  1.87 us

profile of v1, /device:TPU:4, one launch (start us, length us, event | category | flops | bytes accessed | tf_op | source)
XLA Modules:
  0.0 70.2 jit_solution(12834238657558494019)
XLA Ops:
  0.6 1.7 %copy.12.lat_ref = bf16[1,128,576]{2,1,0:T(8,128)(2,1)} copy(bf16[1,128,576]{1,2,0:T(8,128)(2,1)} %param.7) | data formatting | bytes 294912 | tf_op args[0]
  2.3 62.9 %shard_map.110 = (bf16[1,128,512]{2,1,0:T(8,128)(2,1)}, bf16[1,128,512]{2,1,0:T(8,128)(2,1)}, bf16[1,128,256]{2,1,0:T(8,128)(2,1)}, f32[1,128,576]{2,1,0:T(8,128)}, f32[16,128]{1,0:T(8,128)}) custom-call(bf16[1,128,576]{2,1,0:T(8,128)(2,1)} %copy.12.lat_ref, s32[1,1,9]{2,1,0:T(1,128)} %exp_ref.1, bf16[1,128,512]{2,1,0:T(8,128)(2,1)} %qn_ref.1, ...), custom_call_target="tpu_custom_call" | custom-call | tf_op jit(solution)/shard_map/pallas_call | solution.py:637
  65.2 0.0 copy-start.1
  65.3 1.9 %copy.13 = f32[1,128,576]{1,2,0:T(8,128)} copy(f32[1,128,576]{2,1,0:T(8,128)} %get-tuple-element.8) | data formatting | bytes 589824 | tf_op jit(solution)/shard_map/pallas_call | solution.py:637
  67.1 0.0 copy-done.1
  67.1 0.0 copy-start
  67.1 0.7 copy.18
  67.8 0.3 copy-done
  68.1 0.0 copy-start.2
  68.1 0.7 copy.19
  68.7 0.2 copy-done.2
  69.0 0.0 copy-start.3
  69.0 0.6 copy.20
  69.6 0.1 copy-done.3
  69.6 0.6 copy.21
Async XLA Ops:
  65.2 1.9 %copy-start.1 = (bf16[1,128,512]{2,1,0:T(8,128)(2,1)S(1)}, bf16[1,128,512]{2,1,0:T(8,128)(2,1)}, u32[]{:S(2)}) copy-start(bf16[1,128,512]{2,1,0:T(8,128)(2,1)} %get-tuple-element.15) | copy-start | bytes 393220
  67.1 1.0 %copy-start = (bf16[1,128,512]{2,1,0:T(8,128)(2,1)S(1)}, bf16[1,128,512]{2,1,0:T(8,128)(2,1)}, u32[]{:S(2)}) copy-start(bf16[1,128,512]{2,1,0:T(8,128)(2,1)} %get-tuple-element.16) | copy-start | bytes 393220
  68.1 0.9 %copy-start.2 = (bf16[1,128,256]{2,1,0:T(8,128)(2,1)S(1)}, bf16[1,128,256]{2,1,0:T(8,128)(2,1)}, u32[]{:S(2)}) copy-start(bf16[1,128,256]{2,1,0:T(8,128)(2,1)} %get-tuple-element.17) | copy-start | bytes 196612
  69.0 0.7 copy-start.3

commit v2 on v1

v2 whole, which is shorter than its diff:
```python
import math

import jax
import jax.numpy as jnp
from jax import lax
from jax.experimental import pallas as pl
from jax.experimental.pallas import tpu as pltpu
from jax.sharding import PartitionSpec as P

LATENT = 512
ROPE = 64
WIDTH = LATENT + ROPE
HEADS = 4
HEAD = 128
ROWS = 128
HALF = ROWS * HEADS
QROWS = 2 * HALF
Z = 8
KEYS = 2 * ROWS
FACTOR = (HEAD + ROPE) ** -0.5
LOG2E = math.log2(math.e)
NEG = -1e30
SLOTS = 8
NEEDS = (0, 1, 7, 2, 6, 3, 5, 4)
UP_SLOT = (0, 1, 3, 5, 7)
DN_SLOT = (0, 2, 4, 6, 7)
GPARTS = 2
GROWS = WIDTH // GPARTS
TROWS = ROWS + ROWS * ROPE // LATENT
RPARTS = 3
RROWS = TROWS // RPARTS
BF16 = jnp.bfloat16
F32 = jnp.float32


def dot(a, b):
    return jnp.dot(a, b, preferred_element_type=F32)


def transposed(a):
    return a.astype(F32).T.astype(BF16)


def remote(src, dst, send, recv, device):
    return pltpu.make_async_remote_copy(
        src_ref=src,
        dst_ref=dst,
        send_sem=send,
        recv_sem=recv,
        device_id=device,
        device_id_type=pl.DeviceIdType.MESH,
    )


def kernel(
    lat_hbm, exp_ref, qn_hbm, qr_hbm, ku_hbm, vu_hbm, ct_hbm,
    att_ref, gn_ref, gr_ref, gl_ref, gw_ref,
    lat, qn_ref, qr_ref, ku_ref, vu_ref, ct_ref,
    kt, kk, pqn, pqr, pct, q, qt, do, dot_t, kut, vut,
    s_ref, dp_ref, w_ref, ds_ref, acc, dq, ot, dqt, st, pst, fin,
    aown, asend, arecv, gown, gsend, grecv,
    dl, pr, sdn, sup, rdn, rup, tot,
    wg, wa, wb, rb, wc, rc, wd, rd,
    in_sem,
    up_s, up_r, dn_s, dn_r, sib_s, sib_r, pq_s, pq_r, mid_s, mid_r,
    ls_s, ls_r, rdn_s, rdn_r, rup_s, rup_r,
    a_s, a_r, b_s, b_r, c_s, c_r, d_s, d_r,
):
    k = lax.axis_index("ctx")
    p = lax.axis_index("dp")
    z, xh, c = k // 4, lax.rem(k // 2, 2), lax.rem(k, 2)
    y, xl = p // 2, lax.rem(p, 2)
    x = xh * 2 + xl

    def at(z_, x_, c_, y_):
        return (z_ * 4 + (x_ // 2) * 2 + c_, y_ * 2 + lax.rem(x_, 2))

    sibling = at(z, x, 1 - c, y)
    partner = at(z, lax.rem(x + 2, 4), c, y)
    above = at(lax.rem(z + 1, Z), x, c, y)
    below = at(lax.rem(z + Z - 1, Z), x, c, y)
    xpeers = [lax.rem(x + d, 4) for d in (1, 2, 3)]
    ypeers = [lax.rem(y + d, 4) for d in (1, 2, 3)]
    zpeers = [lax.rem(z + d, Z) for d in range(1, Z)]

    loads = [
        pltpu.make_async_copy(src, dst, in_sem.at[i])
        for i, (src, dst) in enumerate((
            (lat_hbm, lat), (ku_hbm, ku_ref), (vu_hbm, vu_ref),
            (qn_hbm, qn_ref), (qr_hbm, qr_ref), (ct_hbm, ct_ref),
        ))
    ]
    for load in loads:
        load.start()

    barrier = pltpu.get_barrier_semaphore()
    peers = [sibling]
    peers += [at(z, v, c, y) for v in xpeers]
    peers += [at(z, x, c, v) for v in ypeers]
    peers += [at(v, x, c, y) for v in zpeers]
    for peer in peers:
        pl.semaphore_signal(barrier, inc=1, device_id=peer, device_id_type=pl.DeviceIdType.MESH)

    st[...] = jnp.zeros_like(st)

    group = lax.broadcasted_iota(jnp.int32, (WIDTH, ROWS), 0) // 64
    exps = jnp.zeros((WIDTH, ROWS), jnp.int32)
    for g in range(WIDTH // 64):
        exps = jnp.where(group == g, exp_ref[0, 0, g], exps)
    scale = jnp.where(exps > 0, 2.0, jnp.where(exps < 0, 0.5, 1.0)).astype(F32)
    loads[0].wait()
    kt[0, c] = (lat[0].astype(F32) * scale).astype(BF16)

    pl.semaphore_wait(barrier, len(peers))

    def piece(h):
        return pl.ds(h * GROWS, GROWS)

    def up_copy(s, h):
        return remote(
            kt.at[UP_SLOT[s - 1], c, piece(h)], kt.at[UP_SLOT[s], c, piece(h)],
            up_s.at[s - 1, h], up_r.at[s - 1, h], above,
        )

    def dn_copy(s, h):
        return remote(
            kt.at[DN_SLOT[s - 1], c, piece(h)], kt.at[DN_SLOT[s], c, piece(h)],
            dn_s.at[s - 1, h], dn_r.at[s - 1, h], below,
        )

    def sib_copy(slot):
        ref = kt.at[slot, c]
        return remote(ref, ref, sib_s.at[slot], sib_r.at[slot], sibling)

    def up_sent(s):
        ok = (z <= Z - 2) & (z >= s - 1)
        return ok & (c == 0) if s == 4 else ok

    def up_got(s):
        return (z >= s) & (c == 0) if s == 4 else z >= s

    def dn_sent(s):
        ok = lax.rem(z + s - 1, Z) <= 2 + c
        return ok & (c == 1) if s == 4 else ok

    def dn_got(s):
        ok = lax.rem(z + s, Z) <= 2 + c
        return ok & (c == 1) if s == 4 else ok

    for h in range(GPARTS):

        @pl.when(up_sent(1))
        def _():
            up_copy(1, h).start()

        @pl.when(dn_sent(1))
        def _():
            dn_copy(1, h).start()

    sib_copy(0).start()
    for load in loads[1:]:
        load.wait()
    query_copies = [
        remote(src.at[0], dst, pq_s.at[i], pq_r.at[i], partner)
        for i, (src, dst) in enumerate(((qn_ref, pqn), (qr_ref, pqr), (ct_ref, pct)))
    ]
    for copy in query_copies:
        copy.start()

    for h in range(HEADS):
        cols = pl.ds(h * HEAD, HEAD)
        kut[cols, :] = transposed(ku_ref[:, cols])
        vut[cols, :] = transposed(vu_ref[:, cols])

    def tables(half, qn, qr, ct):
        rope_t = qr.astype(F32).T
        for h in range(HEADS):
            cols = pl.ds(h * HEAD, HEAD)
            rows = pl.ds(half * HALF + h * HEAD, HEAD)
            qh = qn[:, h * HEAD:(h + 1) * HEAD]
            ch = ct[:, h * HEAD:(h + 1) * HEAD]
            rope_h = rope_t[h * ROPE:(h + 1) * ROPE, :]
            q[rows, pl.ds(0, LATENT)] = dot(qh, kut[cols, :]).astype(BF16)
            q[rows, pl.ds(LATENT, ROPE)] = rope_h.T.astype(BF16)
            qt[pl.ds(0, LATENT), rows] = dot(ku_ref[:, cols], transposed(qh)).astype(BF16)
            qt[pl.ds(LATENT, ROPE), rows] = rope_h.astype(BF16)
            do[rows, :] = dot(ch, vut[cols, :]).astype(BF16)
            dot_t[:, rows] = dot(vu_ref[:, cols], transposed(ch)).astype(BF16)

    tables(0, qn_ref[0], qr_ref[0], ct_ref[0])

    def relay(s):
        for h in range(GPARTS):

            @pl.when(up_got(s))
            def _():
                up_copy(s, h).wait_recv()
                if s < 4:

                    @pl.when(up_sent(s + 1))
                    def _():
                        up_copy(s + 1, h).start()

            @pl.when(dn_got(s))
            def _():
                dn_copy(s, h).wait_recv()
                if s < 4:

                    @pl.when(dn_sent(s + 1))
                    def _():
                        dn_copy(s + 1, h).start()

        for slot in sorted({UP_SLOT[s], DN_SLOT[s]}):

            @pl.when(z >= NEEDS[slot])
            def _():
                sib_copy(slot).start()

    def meet(s):
        for slot in sorted({UP_SLOT[s], DN_SLOT[s]}):

            @pl.when(z >= NEEDS[slot])
            def _():
                sib_copy(slot).wait_recv()
                turn(slot)

    def turn(slot):
        for cc in range(2):
            kk[pl.ds(slot * KEYS + cc * ROWS, ROWS), :] = transposed(kt[slot, cc])

    def columns(slot, count, width):
        return jnp.concatenate(
            [kt[slot + i, cc, :width] for i in range(count) for cc in range(2)], axis=1
        )

    def forward(half, slot, count):
        rows = pl.ds(half * HALF, HALF)
        keys = pl.ds(slot * KEYS, count * KEYS)
        score = dot(kk[keys, :], qt[:, rows]) * (FACTOR * LOG2E)
        if slot == 0:
            kpos = lax.broadcasted_iota(jnp.int32, (KEYS, HALF), 0) + xh * KEYS
            lane = lax.rem(lax.broadcasted_iota(jnp.int32, (KEYS, HALF), 1), ROWS)
            qx = 1 - xh if half else xh
            score = jnp.where(kpos <= lane + (qx * KEYS + c * ROWS), score, NEG)
        dprob = dot(kk[keys, pl.ds(0, LATENT)], dot_t[:, rows])
        s_ref[keys, rows] = score
        dp_ref[keys, rows] = dprob
        top = jnp.max(score, axis=0, keepdims=True)
        if slot:
            old = st[0:1, rows]
            top = jnp.maximum(old, top)
            decay = jnp.exp2(old - top)
        e = jnp.exp2(score - top)
        total = jnp.sum(e, axis=0, keepdims=True)
        delta = jnp.sum(e * dprob, axis=0, keepdims=True)
        mixed = dot(columns(slot, count, LATENT), e.astype(BF16))
        if slot:
            total += st[1:2, rows] * decay
            delta += st[2:3, rows] * decay
            mixed += acc[:, rows] * decay
        st[0:1, rows] = top
        st[1:2, rows] = total
        st[2:3, rows] = delta
        acc[:, rows] = mixed

    def over(slot, work):
        @pl.when(z >= NEEDS[slot + 1])
        def _():
            work(slot, 2)

        @pl.when((z >= NEEDS[slot]) & (z < NEEDS[slot + 1]))
        def _():
            work(slot, 1)

    def both(slot, count):
        forward(0, slot, count)
        forward(1, slot, count)

    sib_copy(0).wait_recv()
    turn(0)
    forward(0, 0, 1)
    relay(1)
    meet(1)
    over(1, lambda slot, count: forward(0, slot, count))
    relay(2)
    for copy in query_copies:
        copy.wait_recv()
    tables(1, pqn[...], pqr[...], pct[...])
    forward(1, 0, 1)
    over(1, lambda slot, count: forward(1, slot, count))
    relay(3)
    meet(2)
    over(3, both)
    relay(4)
    meet(3)
    over(5, both)
    meet(4)

    @pl.when(z >= NEEDS[7])
    def _():
        both(7, 1)

    stats = remote(st, pst, mid_s.at[0], mid_r.at[0], partner)
    stats.start()
    dq[...] = jnp.zeros_like(dq)
    stats.wait_recv()
    for half in range(2):
        rows, other = pl.ds(half * HALF, HALF), pl.ds((1 - half) * HALF, HALF)
        top1, top2 = st[0:1, rows], pst[0:1, other]
        top = jnp.maximum(top1, top2)
        part1, part2 = jnp.exp2(top1 - top), jnp.exp2(top2 - top)
        total = st[1:2, rows] * part1 + pst[1:2, other] * part2
        fin[0:1, rows] = top + jnp.log(total) * LOG2E
        fin[1:2, rows] = (st[2:3, rows] * part1 + pst[2:3, other] * part2) / total
        ot[:, rows] = (acc[:, rows] * (part1 / total)).astype(BF16)

    def store_terms(column, terms):
        yy, xx = column // 2, column % 2
        terms = terms.astype(BF16)
        for zz in range(Z):
            for xxh in range(2):
                for cc in range(2):
                    first = zz * 64 + xxh * 32 + cc * 16
                    wg[cc, yy, xxh * 2 + xx, zz] = terms[first:first + 16, :]

    def backward(slot, count):
        keys = pl.ds(slot * KEYS, count * KEYS)
        cols = columns(slot, count, WIDTH)
        for half in range(2):
            rows = pl.ds(half * HALF, HALF)
            prob = jnp.exp2(s_ref[keys, rows] - fin[0:1, rows])
            w_ref[keys, rows] = prob.astype(BF16)
            dscore = (prob * (dp_ref[keys, rows] - fin[1:2, rows]) * FACTOR).astype(BF16)
            ds_ref[keys, rows] = dscore
            dq[:, rows] += dot(cols, dscore)

    def ls_copy(slot):
        return remote(dl.at[slot, 1 - c], pr.at[slot], ls_s.at[slot], ls_r.at[slot], sibling)

    def latent_terms(slot, count):
        keys = pl.ds(slot * KEYS, count * KEYS)
        a = dot(ds_ref[keys, :], q[...])
        b = dot(w_ref[keys, :], do[...])
        front = (a[:, :LATENT] + b).astype(BF16)
        for i in range(count):
            for cc in range(2):
                first = i * KEYS + cc * ROWS
                dl[slot + i, cc, pl.ds(0, ROWS), :] = front[first:first + ROWS, :]
                rope = a[first:first + ROWS, LATENT:]
                for j in range(4):
                    pair = [rope[j * 32 + n * 16:j * 32 + n * 16 + 16, :] for n in range(2)]
                    dl[slot + i, cc, pl.ds(ROWS, 16), pl.ds(j * 128, 128)] = jnp.concatenate(
                        pair, axis=1
                    ).astype(BF16)
        for i in range(count):
            ls_copy(slot + i).start()

    def strip(h):
        return pl.ds(h * RROWS, RROWS)

    def down_copy(t, h):
        return remote(
            sdn.at[t - 1, strip(h)], rdn.at[t - 1, strip(h)],
            rdn_s.at[t - 1, h], rdn_r.at[t - 1, h], below,
        )

    def rise_copy(t, h, src=None):
        return remote(
            sup.at[t - 1, strip(h)] if src is None else src, rup.at[t - 1, strip(h)],
            rup_s.at[t - 1, h], rup_r.at[t - 1, h], above,
        )

    def chip_sum(slot, h):
        return dl[slot, c, strip(h)].astype(F32) + pr[slot, strip(h)].astype(F32)

    def down_sent(t):
        return (z >= 4) & (c == 0) if t == 1 else z >= 5 - t

    def rise_sent(t):
        ok = lax.rem(z + 5 - t, Z) <= 2 + c
        return ok & (c == 1) if t == 1 else ok

    def pass_on(t):
        down_slot, rise_slot = UP_SLOT[5 - t], DN_SLOT[5 - t]
        for slot in sorted({down_slot, rise_slot}):

            @pl.when(z >= NEEDS[slot])
            def _():
                ls_copy(slot).wait_recv()

        for h in range(RPARTS):

            @pl.when(down_sent(t))
            def _():
                if t == 1:
                    sdn[t - 1, strip(h)] = chip_sum(down_slot, h).astype(BF16)
                else:
                    more = (z <= Z - 2) & (c == 0) if t == 2 else z <= Z - 2

                    @pl.when(more)
                    def _():
                        down_copy(t - 1, h).wait_recv()
                        sdn[t - 1, strip(h)] = (
                            chip_sum(down_slot, h) + rdn[t - 2, strip(h)].astype(F32)
                        ).astype(BF16)

                    @pl.when(jnp.logical_not(more))
                    def _():
                        sdn[t - 1, strip(h)] = chip_sum(down_slot, h).astype(BF16)

                down_copy(t, h).start()

            @pl.when(rise_sent(t))
            def _():
                if t == 1:
                    sup[t - 1, strip(h)] = chip_sum(rise_slot, h).astype(BF16)
                    rise_copy(t, h).start()
                else:
                    more = c == 1 if t == 2 else c >= 0
                    adds = z >= t + 3

                    @pl.when(more)
                    def _():
                        rise_copy(t - 1, h).wait_recv()

                    @pl.when(adds & more)
                    def _():
                        sup[t - 1, strip(h)] = (
                            chip_sum(rise_slot, h) + rup[t - 2, strip(h)].astype(F32)
                        ).astype(BF16)
                        rise_copy(t, h).start()

                    @pl.when(adds & jnp.logical_not(more))
                    def _():
                        sup[t - 1, strip(h)] = chip_sum(rise_slot, h).astype(BF16)
                        rise_copy(t, h).start()

                    @pl.when(jnp.logical_not(adds))
                    def _():
                        rise_copy(t, h, rup.at[t - 2, strip(h)]).start()

    def chain(slot, count):
        backward(slot, count)
        latent_terms(slot, count)

    def sides(h):
        return pl.ds(h * HEAD, HEAD), pl.ds(HALF + h * HEAD, HEAD)

    a_copies = [
        remote(wg.at[1 - c, pl.ds(2 * i, 2)], wa.at[pl.ds(2 * i, 2)], a_s.at[i], a_r.at[i], sibling)
        for i in range(2)
    ]

    def b_copy(v):
        return remote(wb.at[v], rb.at[y], b_s.at[v], b_r.at[y], at(z, x, c, v))

    def b_wait(v):
        return remote(wb.at[v], rb.at[v], b_s.at[v], b_r.at[v], at(z, x, c, v))

    def chip_weights(i):
        a_copies[i].wait_recv()
        for v in (2 * i, 2 * i + 1):
            wb[v] = (wg[c, v].astype(F32) + wa[v].astype(F32)).astype(BF16)

            @pl.when(y != v)
            def _():
                b_copy(v).start()

    c_copies = [
        remote(wc.at[v], rc.at[i], c_s.at[i], c_r.at[i], at(z, v, c, y))
        for i, v in enumerate(xpeers)
    ]
    d_copies = [
        remote(wd.at[v], rd.at[i], d_s.at[i], d_r.at[i], at(v, x, c, y))
        for i, v in enumerate(zpeers)
    ]

    def row_weights():
        for v in ypeers:
            b_wait(v).wait_recv()
        wc[...] = (
            wb[y].astype(F32) + rb[ypeers[0]].astype(F32)
            + rb[ypeers[1]].astype(F32) + rb[ypeers[2]].astype(F32)
        ).astype(BF16)
        for copy in c_copies:
            copy.start()

    def column_weights():
        for copy in c_copies:
            copy.wait_recv()
        wd[...] = (
            wc[x].astype(F32) + rc[0].astype(F32) + rc[1].astype(F32) + rc[2].astype(F32)
        ).astype(BF16)
        for copy in d_copies:
            copy.start()

    def value_terms():
        for h in range(HEADS):
            cols = pl.ds(h * HEAD, HEAD)
            mine, theirs = sides(h)
            store_terms(
                4 + h, dot(ot[:, mine], ct_ref[0, :, cols]) + dot(ot[:, theirs], pct[:, cols])
            )
        a_copies[1].start()

    def key_terms():
        dqt[...] = dq[pl.ds(0, LATENT), :].astype(BF16)
        for h in range(HEADS):
            cols = pl.ds(h * HEAD, HEAD)
            mine, theirs = sides(h)
            store_terms(
                h, dot(dqt[:, mine], qn_ref[0, :, cols]) + dot(dqt[:, theirs], pqn[:, cols])
            )
        a_copies[0].start()

    att_copy = remote(asend, arecv, mid_s.at[1], mid_r.at[1], partner)
    grad_copy = remote(gsend, grecv, mid_s.at[2], mid_r.at[2], partner)

    def share_output():
        for h in range(HEADS):
            cols = pl.ds(h * HEAD, HEAD)
            mine, theirs = sides(h)
            asend[cols, :] = dot(vut[cols, :], ot[:, theirs]).astype(BF16)
            aown[cols, :] = dot(vut[cols, :], ot[:, mine])
        att_copy.start()

    def share_grads():
        for h in range(HEADS):
            cols = pl.ds(h * HEAD, HEAD)
            rope = pl.ds(LATENT + h * ROPE, ROPE)
            mine, theirs = sides(h)
            gsend[cols, :] = dot(kut[cols, :], dqt[:, theirs]).astype(BF16)
            gown[cols, :] = dot(kut[cols, :], dqt[:, mine])
            gsend[rope, :] = dq[pl.ds(LATENT, ROPE), theirs].astype(BF16)
            gown[rope, :] = dq[pl.ds(LATENT, ROPE), mine]
        grad_copy.start()

    @pl.when(z >= NEEDS[7])
    def _():
        chain(7, 1)

    over(5, backward)
    over(3, backward)
    pass_on(1)
    over(1, backward)
    backward(0, 1)
    key_terms()
    value_terms()
    over(5, latent_terms)
    chip_weights(0)
    chip_weights(1)
    share_output()
    share_grads()
    pass_on(2)
    over(3, latent_terms)
    over(1, latent_terms)
    latent_terms(0, 1)
    pass_on(3)
    row_weights()
    pass_on(4)
    column_weights()

    att_copy.wait_recv()
    grad_copy.wait_recv()
    for h in range(HEADS):
        cols = pl.ds(h * HEAD, HEAD)
        att_ref[0, :, cols] = (aown[cols, :] + arecv[cols, :].astype(F32)).T.astype(BF16)
        gn_ref[0, :, cols] = (gown[cols, :] + grecv[cols, :].astype(F32)).T.astype(BF16)
    for h in range(HEADS // 2):
        rows = pl.ds(LATENT + h * HEAD, HEAD)
        cols = pl.ds(h * HEAD, HEAD)
        gr_ref[0, :, cols] = (gown[rows, :] + grecv[rows, :].astype(F32)).T.astype(BF16)

    for copy in d_copies:
        copy.wait_recv()
    summed = wd[z].astype(F32)
    for i in range(Z - 1):
        summed += rd[i].astype(F32)
    gw_ref[...] = summed

    ls_copy(0).wait_recv()
    for h in range(RPARTS):
        tot[strip(h), :] = chip_sum(0, h)

        @pl.when(z <= Z - 2)
        def _():
            down_copy(4, h).wait_recv()
            tot[strip(h), :] += rdn[3, strip(h)].astype(F32)

        @pl.when(z <= 2 + c)
        def _():
            rise_copy(4, h).wait_recv()
            tot[strip(h), :] += rup[3, strip(h)].astype(F32)

    folded = tot[pl.ds(ROWS, 16), :]
    rope = jnp.concatenate(
        [folded[:, j * ROPE:(j + 1) * ROPE] for j in range(LATENT // ROPE)], axis=0
    )
    gl_ref[0, pl.ds(0, LATENT), :] = tot[pl.ds(0, ROWS), :].T * scale[:LATENT, :]
    gl_ref[0, pl.ds(LATENT, ROPE), :] = rope.T * scale[LATENT:, :]

    for s in range(1, 5):
        for h in range(GPARTS):

            @pl.when(up_sent(s))
            def _():
                up_copy(s, h).wait_send()

            @pl.when(dn_sent(s))
            def _():
                dn_copy(s, h).wait_send()

        for h in range(RPARTS):

            @pl.when(down_sent(s))
            def _():
                down_copy(s, h).wait_send()

            @pl.when(rise_sent(s))
            def _():
                rise_copy(s, h).wait_send()

    for slot in range(SLOTS):

        @pl.when(z >= NEEDS[slot])
        def _():
            sib_copy(slot).wait_send()
            ls_copy(slot).wait_send()

    for v in range(4):

        @pl.when(y != v)
        def _():
            b_copy(v).wait_send()

    for copy in query_copies + [stats, att_copy, grad_copy] + a_copies + c_copies + d_copies:
        copy.wait_send()


def shards(latent_values, latent_exponents, query_nope, query_rope, key_up, value_up, cotangent):
    dma = pltpu.SemaphoreType.DMA
    vmem = pl.BlockSpec(memory_space=pltpu.VMEM)
    scratch = [
        ((1, WIDTH, ROWS), BF16),
        ((1, ROWS, HALF), BF16),
        ((1, ROWS, HALF // 2), BF16),
        ((LATENT, HALF), BF16),
        ((LATENT, HALF), BF16),
        ((1, ROWS, HALF), BF16),
        ((SLOTS, 2, WIDTH, ROWS), BF16),
        ((SLOTS * KEYS, WIDTH), BF16),
        ((ROWS, HALF), BF16),
        ((ROWS, HALF // 2), BF16),
        ((ROWS, HALF), BF16),
        ((QROWS, WIDTH), BF16),
        ((WIDTH, QROWS), BF16),
        ((QROWS, LATENT), BF16),
        ((LATENT, QROWS), BF16),
        ((HALF, LATENT), BF16),
        ((HALF, LATENT), BF16),
        ((SLOTS * KEYS, QROWS), F32),
        ((SLOTS * KEYS, QROWS), F32),
        ((SLOTS * KEYS, QROWS), BF16),
        ((SLOTS * KEYS, QROWS), BF16),
        ((LATENT, QROWS), F32),
        ((WIDTH, QROWS), F32),
        ((LATENT, QROWS), BF16),
        ((LATENT, QROWS), BF16),
        ((8, QROWS), F32),
        ((8, QROWS), F32),
        ((8, QROWS), F32),
        ((HALF, ROWS), F32),
        ((HALF, ROWS), BF16),
        ((HALF, ROWS), BF16),
        ((HALF + HALF // 2, ROWS), F32),
        ((HALF + HALF // 2, ROWS), BF16),
        ((HALF + HALF // 2, ROWS), BF16),
        ((SLOTS, 2, TROWS, LATENT), BF16),
        ((SLOTS, TROWS, LATENT), BF16),
        ((4, TROWS, LATENT), BF16),
        ((4, TROWS, LATENT), BF16),
        ((4, TROWS, LATENT), BF16),
        ((4, TROWS, LATENT), BF16),
        ((TROWS, LATENT), F32),
        ((2, 4, 4, Z, 16, 128), BF16),
        ((4, 4, Z, 16, 128), BF16),
        ((4, 4, Z, 16, 128), BF16),
        ((4, 4, Z, 16, 128), BF16),
        ((4, Z, 16, 128), BF16),
        ((3, Z, 16, 128), BF16),
        ((Z, 16, 128), BF16),
        ((Z - 1, 16, 128), BF16),
    ]
    pairs = [
        (4, GPARTS), (4, GPARTS), (SLOTS,), (3,), (3,),
        (SLOTS,), (4, RPARTS), (4, RPARTS),
        (2,), (4,), (3,), (Z - 1,),
    ]
    semaphores = [dma((6,))]
    for shape in pairs:
        semaphores += [dma(shape)] * 2
    hbm = pl.BlockSpec(memory_space=pl.ANY)
    outs = pl.pallas_call(
        kernel,
        out_shape=(
            jax.ShapeDtypeStruct((1, ROWS, HALF), BF16),
            jax.ShapeDtypeStruct((1, ROWS, HALF), BF16),
            jax.ShapeDtypeStruct((1, ROWS, HALF // 2), BF16),
            jax.ShapeDtypeStruct((1, WIDTH, ROWS), F32),
            jax.ShapeDtypeStruct((16, 128), F32),
        ),
        in_specs=[hbm, pl.BlockSpec(memory_space=pltpu.SMEM)] + [hbm] * 5,
        out_specs=(vmem,) * 5,
        scratch_shapes=[pltpu.VMEM(*spec) for spec in scratch] + semaphores,
        compiler_params=pltpu.CompilerParams(
            collective_id=0, has_side_effects=True, vmem_limit_bytes=60 << 20
        ),
    )(
        jnp.swapaxes(latent_values, 1, 2), latent_exponents,
        query_nope, query_rope, key_up, value_up, cotangent,
    )
    return outs[:3] + (jnp.swapaxes(outs[3], 1, 2), outs[4])


def solution(mesh):
    block = P("dp", "ctx", None)
    return jax.shard_map(
        shards,
        mesh=mesh,
        in_specs=(block, block, block, block, P(), P(), block),
        out_specs=(block, block, block, block, P("ctx", "dp")),
        check_vma=False,
    )
```

time: 70.9 us -> 64.2 us (0.906)
  Pallas kernels: 62.9 us -> 58.9 us
  local copies, waits for them, and re-layouts: 6.7 us -> 4.43 us
    pallas_call x1, Pallas kernels: 62.9 us -> 58.9 us  [shards(): pl.pallas_call(kernel, out_shape=(jax.ShapeDtypeStruct((1, ROWS, HALF), B...]
    pallas_call x1 -> x0, local copies, waits for them, and re-layouts: 1.87 us -> none  [shards(): pl.pallas_call(kernel, out_shape=(jax.ShapeDtypeStruct((1, ROWS, HALF), B...]
where the time goes in v2:
time: 64.2 us; the launch traced here: 64 us
  Pallas kernels  58.9 us (92%)
  local copies, waits for them, and re-layouts  4.43 us (7%)
  between operations  0.66 us (1%)
    pallas_call x1, Pallas kernels, shards(): pl.pallas_call(kernel, out_shape=(jax.ShapeDtypeStruct((1, ROWS, HALF), B...  58.9 us
    unnamed x13, local copies, waits for them, and re-layouts  4.43 us

profile of v2, /device:TPU:4, one launch (start us, length us, event | category | flops | bytes accessed | tf_op | source)
XLA Modules:
  0.0 64.0 jit_solution(14632070562798991517)
XLA Ops:
  0.6 58.9 %shard_map.110 = (bf16[1,128,512]{2,1,0:T(8,128)(2,1)}, bf16[1,128,512]{2,1,0:T(8,128)(2,1)}, bf16[1,128,256]{2,1,0:T(8,128)(2,1)}, f32[1,576,128]{2,1,0:T(8,128)}, f32[16,128]{1,0:T(8,128)}) custom-call(bf16[1,576,128]{2,1,0:T(8,128)(2,1)} %bitcast.3, s32[1,1,9]{2,1,0:T(1,128)} %exp_ref.1, bf16[1,128,512]{2,1,0:T(8,128)(2,1)} %qn_hbm.1, ...), custom_call_target="tpu_custom_call" | custom-call | tf_op jit(solution)/shard_map/pallas_call | solution.py:703
  59.6 0.0 copy-start.1
  59.6 0.0 copy-start
  59.6 1.6 %copy.17 = bf16[1,128,512]{2,1,0:T(8,128)(2,1)} copy(bf16[1,128,512]{2,1,0:T(8,128)(2,1)} %get-tuple-element.20) | data formatting | bytes 262144
  61.2 0.0 copy-done.1
  61.2 0.0 copy-start.2
  61.2 0.7 %copy.18 = bf16[1,128,512]{2,1,0:T(8,128)(2,1)} copy(bf16[1,128,512]{2,1,0:T(8,128)(2,1)S(1)} %copy-done.1) | data formatting | bytes 262144
  61.9 0.2 copy-done.2
  62.1 0.6 copy.19
  62.7 0.0 copy-done
  62.7 0.0 copy-start.3
  62.7 0.7 %copy.20 = f32[1,128,576]{1,2,0:T(8,128)} copy(f32[1,128,576]{1,2,0:T(8,128)S(1)} %bitcast.2) | data formatting | bytes 589824
  63.4 0.0 copy-done.3
  63.4 0.6 copy.21
Async XLA Ops:
  59.6 1.6 %copy-start.1 = (bf16[1,128,512]{2,1,0:T(8,128)(2,1)S(1)}, bf16[1,128,512]{2,1,0:T(8,128)(2,1)}, u32[]{:S(2)}) copy-start(bf16[1,128,512]{2,1,0:T(8,128)(2,1)} %get-tuple-element.21) | copy-start | bytes 393220
  59.6 3.1 %copy-start = (f32[1,576,128]{2,1,0:T(8,128)S(1)}, f32[1,576,128]{2,1,0:T(8,128)}, u32[]{:S(2)}) copy-start(f32[1,576,128]{2,1,0:T(8,128)} %get-tuple-element.13) | copy-start | bytes 884740
  61.2 0.9 %copy-start.2 = (bf16[1,128,256]{2,1,0:T(8,128)(2,1)S(1)}, bf16[1,128,256]{2,1,0:T(8,128)(2,1)}, u32[]{:S(2)}) copy-start(bf16[1,128,256]{2,1,0:T(8,128)(2,1)} %get-tuple-element.22) | copy-start | bytes 196612
  62.7 0.7 %copy-start.3 = (f32[16,128]{1,0:T(8,128)S(1)}, f32[16,128]{1,0:T(8,128)}, u32[]{:S(2)}) copy-start(f32[16,128]{1,0:T(8,128)} %get-tuple-element.24) | copy-start | bytes 24580

commit v3 on v2

--- a/solution.py
+++ b/solution.py
@@ -24,7 +24,7 @@
 NEEDS = (0, 1, 7, 2, 6, 3, 5, 4)
 UP_SLOT = (0, 1, 3, 5, 7)
 DN_SLOT = (0, 2, 4, 6, 7)
-GPARTS = 2
+GPARTS = 3
 GROWS = WIDTH // GPARTS
 TROWS = ROWS + ROWS * ROPE // LATENT
 RPARTS = 3
@@ -90,16 +90,18 @@
             (qn_hbm, qn_ref), (qr_hbm, qr_ref), (ct_hbm, ct_ref),
         ))
     ]
-    for load in loads:
-        load.start()
+    loads[0].start()
 
     barrier = pltpu.get_barrier_semaphore()
-    peers = [sibling]
+    peers = [at(lax.rem(z + d, Z), x, c, y) for d in (4, 3, 5, 2, 6, 1, 7)]
     peers += [at(z, v, c, y) for v in xpeers]
     peers += [at(z, x, c, v) for v in ypeers]
-    peers += [at(v, x, c, y) for v in zpeers]
+    peers += [sibling]
     for peer in peers:
         pl.semaphore_signal(barrier, inc=1, device_id=peer, device_id_type=pl.DeviceIdType.MESH)
+
+    for load in loads[1:]:
+        load.start()
 
     st[...] = jnp.zeros_like(st)
 
@@ -119,13 +121,13 @@
     def up_copy(s, h):
         return remote(
             kt.at[UP_SLOT[s - 1], c, piece(h)], kt.at[UP_SLOT[s], c, piece(h)],
-            up_s.at[s - 1, h], up_r.at[s - 1, h], above,
+            up_s.at[s - 1], up_r.at[s - 1, h], above,
         )
 
     def dn_copy(s, h):
         return remote(
             kt.at[DN_SLOT[s - 1], c, piece(h)], kt.at[DN_SLOT[s], c, piece(h)],
-            dn_s.at[s - 1, h], dn_r.at[s - 1, h], below,
+            dn_s.at[s - 1], dn_r.at[s - 1, h], below,
         )
 
     def sib_copy(slot):
@@ -167,25 +169,24 @@
     for copy in query_copies:
         copy.start()
 
-    for h in range(HEADS):
-        cols = pl.ds(h * HEAD, HEAD)
-        kut[cols, :] = transposed(ku_ref[:, cols])
-        vut[cols, :] = transposed(vu_ref[:, cols])
-
     def tables(half, qn, qr, ct):
-        rope_t = qr.astype(F32).T
+        rope_t = qr.astype(F32).T.astype(BF16)
         for h in range(HEADS):
             cols = pl.ds(h * HEAD, HEAD)
             rows = pl.ds(half * HALF + h * HEAD, HEAD)
             qh = qn[:, h * HEAD:(h + 1) * HEAD]
             ch = ct[:, h * HEAD:(h + 1) * HEAD]
-            rope_h = rope_t[h * ROPE:(h + 1) * ROPE, :]
-            q[rows, pl.ds(0, LATENT)] = dot(qh, kut[cols, :]).astype(BF16)
-            q[rows, pl.ds(LATENT, ROPE)] = rope_h.T.astype(BF16)
             qt[pl.ds(0, LATENT), rows] = dot(ku_ref[:, cols], transposed(qh)).astype(BF16)
-            qt[pl.ds(LATENT, ROPE), rows] = rope_h.astype(BF16)
-            do[rows, :] = dot(ch, vut[cols, :]).astype(BF16)
+            qt[pl.ds(LATENT, ROPE), rows] = rope_t[h * ROPE:(h + 1) * ROPE, :]
             dot_t[:, rows] = dot(vu_ref[:, cols], transposed(ch)).astype(BF16)
+
+    def row_tables(half, qn, ct):
+        for h in range(HEADS):
+            cols = pl.ds(h * HEAD, HEAD)
+            rows = pl.ds(half * HALF + h * HEAD, HEAD)
+            q[rows, pl.ds(0, LATENT)] = dot(qn[:, h * HEAD:(h + 1) * HEAD], kut[cols, :]).astype(BF16)
+            q[rows, pl.ds(LATENT, ROPE)] = transposed(qt[pl.ds(LATENT, ROPE), rows])
+            do[rows, :] = dot(ct[:, h * HEAD:(h + 1) * HEAD], vut[cols, :]).astype(BF16)
 
     tables(0, qn_ref[0], qr_ref[0], ct_ref[0])
 
@@ -302,6 +303,13 @@
 
     stats = remote(st, pst, mid_s.at[0], mid_r.at[0], partner)
     stats.start()
+    for h in range(HEADS):
+        cols = pl.ds(h * HEAD, HEAD)
+        kut[cols, :] = transposed(ku_ref[:, cols])
+        vut[cols, :] = transposed(vu_ref[:, cols])
+
+    row_tables(0, qn_ref[0], ct_ref[0])
+    row_tables(1, pqn[...], pct[...])
     dq[...] = jnp.zeros_like(dq)
     stats.wait_recv()
     for half in range(2):
@@ -312,7 +320,7 @@
         total = st[1:2, rows] * part1 + pst[1:2, other] * part2
         fin[0:1, rows] = top + jnp.log(total) * LOG2E
         fin[1:2, rows] = (st[2:3, rows] * part1 + pst[2:3, other] * part2) / total
-        ot[:, rows] = (acc[:, rows] * (part1 / total)).astype(BF16)
+        fin[2:3, rows] = part1 / total
 
     def store_terms(column, terms):
         yy, xx = column // 2, column % 2
@@ -361,13 +369,13 @@
     def down_copy(t, h):
         return remote(
             sdn.at[t - 1, strip(h)], rdn.at[t - 1, strip(h)],
-            rdn_s.at[t - 1, h], rdn_r.at[t - 1, h], below,
+            rdn_s.at[t - 1], rdn_r.at[t - 1, h], below,
         )
 
     def rise_copy(t, h, src=None):
         return remote(
             sup.at[t - 1, strip(h)] if src is None else src, rup.at[t - 1, strip(h)],
-            rup_s.at[t - 1, h], rup_r.at[t - 1, h], above,
+            rup_s.at[t - 1], rup_r.at[t - 1, h], above,
         )
 
     def chip_sum(slot, h):
@@ -452,10 +460,10 @@
     ]
 
     def b_copy(v):
-        return remote(wb.at[v], rb.at[y], b_s.at[v], b_r.at[y], at(z, x, c, v))
-
-    def b_wait(v):
-        return remote(wb.at[v], rb.at[v], b_s.at[v], b_r.at[v], at(z, x, c, v))
+        return remote(wb.at[v], rb.at[y], b_s.at[0], b_r.at[0], at(z, x, c, v))
+
+    three = pl.ds(0, 3)
+    b_all = remote(wb.at[three], rb.at[three], b_s.at[0], b_r.at[0], above)
 
     def chip_weights(i):
         a_copies[i].wait_recv()
@@ -467,17 +475,17 @@
                 b_copy(v).start()
 
     c_copies = [
-        remote(wc.at[v], rc.at[i], c_s.at[i], c_r.at[i], at(z, v, c, y))
+        remote(wc.at[v], rc.at[i], c_s.at[0], c_r.at[0], at(z, v, c, y))
         for i, v in enumerate(xpeers)
     ]
+    c_all = remote(wc.at[three], rc.at[three], c_s.at[0], c_r.at[0], partner)
     d_copies = [
-        remote(wd.at[v], rd.at[i], d_s.at[i], d_r.at[i], at(v, x, c, y))
+        remote(wd.at[v], rd.at[i], d_s.at[0], d_r.at[0], at(v, x, c, y))
         for i, v in enumerate(zpeers)
     ]
 
     def row_weights():
-        for v in ypeers:
-            b_wait(v).wait_recv()
+        b_all.wait_recv()
         wc[...] = (
             wb[y].astype(F32) + rb[ypeers[0]].astype(F32)
             + rb[ypeers[1]].astype(F32) + rb[ypeers[2]].astype(F32)
@@ -486,8 +494,7 @@
             copy.start()
 
     def column_weights():
-        for copy in c_copies:
-            copy.wait_recv()
+        c_all.wait_recv()
         wd[...] = (
             wc[x].astype(F32) + rc[0].astype(F32) + rc[1].astype(F32) + rc[2].astype(F32)
         ).astype(BF16)
@@ -540,15 +547,16 @@
         chain(7, 1)
 
     over(5, backward)
+    ot[...] = (acc[...] * fin[2:3, :]).astype(BF16)
+    value_terms()
     over(3, backward)
     pass_on(1)
     over(1, backward)
     backward(0, 1)
     key_terms()
-    value_terms()
+    chip_weights(1)
     over(5, latent_terms)
     chip_weights(0)
-    chip_weights(1)
     share_output()
     share_grads()
     pass_on(2)
@@ -571,8 +579,9 @@
         cols = pl.ds(h * HEAD, HEAD)
         gr_ref[0, :, cols] = (gown[rows, :] + grecv[rows, :].astype(F32)).T.astype(BF16)
 
-    for copy in d_copies:
-        copy.wait_recv()
+    every = pl.ds(0, Z - 1)
+    d_all = remote(wd.at[every], rd.at[every], d_s.at[0], d_r.at[0], above)
+    d_all.wait_recv()
     summed = wd[z].astype(F32)
     for i in range(Z - 1):
         summed += rd[i].astype(F32)
@@ -600,25 +609,26 @@
     gl_ref[0, pl.ds(LATENT, ROPE), :] = rope.T * scale[LATENT:, :]
 
     for s in range(1, 5):
-        for h in range(GPARTS):
-
-            @pl.when(up_sent(s))
-            def _():
-                up_copy(s, h).wait_send()
-
-            @pl.when(dn_sent(s))
-            def _():
-                dn_copy(s, h).wait_send()
-
-        for h in range(RPARTS):
-
-            @pl.when(down_sent(s))
-            def _():
-                down_copy(s, h).wait_send()
-
-            @pl.when(rise_sent(s))
-            def _():
-                rise_copy(s, h).wait_send()
+
+        @pl.when(up_sent(s))
+        def _():
+            remote(kt.at[0, 0], kt.at[0, 0], up_s.at[s - 1], up_r.at[s - 1, 0], above).wait_send()
+
+        @pl.when(dn_sent(s))
+        def _():
+            remote(kt.at[0, 0], kt.at[0, 0], dn_s.at[s - 1], dn_r.at[s - 1, 0], below).wait_send()
+
+        @pl.when(down_sent(s))
+        def _():
+            remote(
+                sdn.at[s - 1], rdn.at[s - 1], rdn_s.at[s - 1], rdn_r.at[s - 1, 0], below
+            ).wait_send()
+
+        @pl.when(rise_sent(s))
+        def _():
+            remote(
+                sup.at[s - 1], rup.at[s - 1], rup_s.at[s - 1], rup_r.at[s - 1, 0], above
+            ).wait_send()
 
     for slot in range(SLOTS):
 
@@ -627,13 +637,9 @@
             sib_copy(slot).wait_send()
             ls_copy(slot).wait_send()
 
-    for v in range(4):
-
-        @pl.when(y != v)
-        def _():
-            b_copy(v).wait_send()
-
-    for copy in query_copies + [stats, att_copy, grad_copy] + a_copies + c_copies + d_copies:
+    b_all.wait_send()
+
+    for copy in query_copies + [stats, att_copy, grad_copy] + a_copies + [c_all, d_all]:
         copy.wait_send()
 
 
@@ -692,13 +698,13 @@
         ((Z - 1, 16, 128), BF16),
     ]
     pairs = [
-        (4, GPARTS), (4, GPARTS), (SLOTS,), (3,), (3,),
-        (SLOTS,), (4, RPARTS), (4, RPARTS),
-        (2,), (4,), (3,), (Z - 1,),
+        ((4,), (4, GPARTS)), ((4,), (4, GPARTS)), ((SLOTS,),) * 2, ((3,),) * 2, ((3,),) * 2,
+        ((SLOTS,),) * 2, ((4,), (4, RPARTS)), ((4,), (4, RPARTS)),
+        ((2,),) * 2, ((1,),) * 2, ((1,),) * 2, ((1,),) * 2,
     ]
     semaphores = [dma((6,))]
-    for shape in pairs:
-        semaphores += [dma(shape)] * 2
+    for sent, received in pairs:
+        semaphores += [dma(sent), dma(received)]
     hbm = pl.BlockSpec(memory_space=pl.ANY)
     outs = pl.pallas_call(
         kernel,

time: 64.2 us -> 63.6 us (level)
  no operation moved by 1% of the time
where the time goes in v3:
time: 63.6 us; the launch traced here: 63.4 us
  Pallas kernels  58.3 us (92%)
  local copies, waits for them, and re-layouts  4.43 us (7%)
  between operations  0.66 us (1%)
    pallas_call x1, Pallas kernels, shards(): pl.pallas_call(kernel, out_shape=(jax.ShapeDtypeStruct((1, ROWS, HALF), B...  58.3 us
    unnamed x13, local copies, waits for them, and re-layouts  4.43 us

profile of v3, /device:TPU:4, one launch (start us, length us, event | category | flops | bytes accessed | tf_op | source)
XLA Modules:
  0.0 63.4 jit_solution(11293729153995013619)
XLA Ops:
  0.6 58.3 %shard_map.110 = (bf16[1,128,512]{2,1,0:T(8,128)(2,1)}, bf16[1,128,512]{2,1,0:T(8,128)(2,1)}, bf16[1,128,256]{2,1,0:T(8,128)(2,1)}, f32[1,576,128]{2,1,0:T(8,128)}, f32[16,128]{1,0:T(8,128)}) custom-call(bf16[1,576,128]{2,1,0:T(8,128)(2,1)} %bitcast.3, s32[1,1,9]{2,1,0:T(1,128)} %exp_ref.1, bf16[1,128,512]{2,1,0:T(8,128)(2,1)} %qn_hbm.1, ...), custom_call_target="tpu_custom_call" | custom-call | tf_op jit(solution)/shard_map/pallas_call | solution.py:709
  59.0 0.0 copy-start.1
  59.0 0.0 copy-start
  59.0 1.6 %copy.17 = bf16[1,128,512]{2,1,0:T(8,128)(2,1)} copy(bf16[1,128,512]{2,1,0:T(8,128)(2,1)} %get-tuple-element.20) | data formatting | bytes 262144
  60.6 0.0 copy-done.1
  60.6 0.0 copy-start.2
  60.6 0.7 %copy.18 = bf16[1,128,512]{2,1,0:T(8,128)(2,1)} copy(bf16[1,128,512]{2,1,0:T(8,128)(2,1)S(1)} %copy-done.1) | data formatting | bytes 262144
  61.3 0.2 copy-done.2
  61.5 0.6 copy.19
  62.1 0.0 copy-done
  62.1 0.0 copy-start.3
  62.1 0.7 %copy.20 = f32[1,128,576]{1,2,0:T(8,128)} copy(f32[1,128,576]{1,2,0:T(8,128)S(1)} %bitcast.2) | data formatting | bytes 589824
  62.8 0.0 copy-done.3
  62.8 0.6 copy.21
Async XLA Ops:
  59.0 1.6 %copy-start.1 = (bf16[1,128,512]{2,1,0:T(8,128)(2,1)S(1)}, bf16[1,128,512]{2,1,0:T(8,128)(2,1)}, u32[]{:S(2)}) copy-start(bf16[1,128,512]{2,1,0:T(8,128)(2,1)} %get-tuple-element.21) | copy-start | bytes 393220
  59.0 3.1 %copy-start = (f32[1,576,128]{2,1,0:T(8,128)S(1)}, f32[1,576,128]{2,1,0:T(8,128)}, u32[]{:S(2)}) copy-start(f32[1,576,128]{2,1,0:T(8,128)} %get-tuple-element.13) | copy-start | bytes 884740
  60.6 0.9 %copy-start.2 = (bf16[1,128,256]{2,1,0:T(8,128)(2,1)S(1)}, bf16[1,128,256]{2,1,0:T(8,128)(2,1)}, u32[]{:S(2)}) copy-start(bf16[1,128,256]{2,1,0:T(8,128)(2,1)} %get-tuple-element.22) | copy-start | bytes 196612
  62.1 0.7 %copy-start.3 = (f32[16,128]{1,0:T(8,128)S(1)}, f32[16,128]{1,0:T(8,128)}, u32[]{:S(2)}) copy-start(f32[16,128]{1,0:T(8,128)} %get-tuple-element.24) | copy-start | bytes 24580
